TPU v7x, 32 devices: a whole 2x2x4 slice. The times are simulated.
32 devices in a mesh: scen: 8 (over y, x, core), space: 2 (over z_hi), tm: 2 (over z_lo).
Axes of the slice: x: 2, y: 2, z: 4 (z_hi: 2, z_lo: 2; z = z_hi * 2 + z_lo), core: 2. Of those that a mesh axis runs over, the one named last changes fastest.
Arguments:
- coupling: bfloat16 [8, 4, 2, 128, 512], P('scen', 'tm', 'space'), may hold values from -0.1875 to 0.1875
- leaf_rhs: float32 [8, 4, 2, 128], P('scen', 'tm', 'space'), may hold values from -6 to 6
- conductance: float32 [8, 4, 2, 128], P('scen', 'tm', 'space'), may hold values from 0.42 to 0.52
- compressor: int32 [8, 4, 2], P('scen', 'tm', 'space'), may hold values 0 or 1
- blocks: float32 [8, 4, 2, 128, 128], P('scen', 'tm', 'space'), may hold values from -2 to 8, as said below
- parent_of: int32 [8], P('scen'), may hold values from 0 to 7, as said below
- parent_mat: float32 [8, 512, 512], P(None, ('space', 'tm')), may hold values from -2 to 8, as said below
- parent_rhs: float32 [8, 512], P(None, ('space', 'tm')), may hold values from -6 to 6
- link: float32 [8, 512, 256], P(None, ('space', 'tm')), may hold values from -0.25 to 0.25
- root_mat: float32 [256, 256], replicated, may hold values from -2 to 8, as said below
- root_rhs: float32 [256], replicated, may hold values from -6 to 6
Outputs:
- leaf_move: float32 [8, 4, 2, 128], P('scen', 'tm', 'space')
- parent_at_leaf: float32 [8, 512], P('scen', ('space', 'tm'))
- root_step: float32 [256], replicated
Inputs may be any that keep to these rules, and one draw needn't show every extreme that they name: `parent_of`: leaves come in aligned runs of 1 in a row; all leaves of a run share one parent, and each parent owns exactly one run. `blocks`: each block is symmetric with eigenvalues of 1 or more. `parent_mat`: each matrix is symmetric with eigenvalues of 1 or more. `root_mat`: symmetric with eigenvalues of 1 or more.
All inputs are finite; a program needn't handle non-finite values. No bound on the sum of `compressor` on one device may be relied on, other than what follows from the above.
Results may differ from a plain program's by a relative error of at most 0.0003.
Values sent between devices are 32-bit elements; how exact they have to be, the bound alone decides.
A program may use at most 64 MiB of HBM per device.

v0:
```python
import jax
import jax.numpy as jnp
from jax import lax
from jax.sharding import PartitionSpec as P

PARENTS = 8
ITERS = 6


HIGH = lax.Precision.HIGHEST


def extended(cells, sides, width):
    for axis, dim in sides:
        count = lax.axis_size(axis)
        ends = count - 1
        head = lax.slice_in_dim(cells, 0, width, axis=dim)
        tail = lax.slice_in_dim(cells, cells.shape[dim] - width, cells.shape[dim], axis=dim)
        cells = jnp.concatenate(
            [
                lax.ppermute(tail, axis, [(i, (i + 1) % count) for i in range(ends)]),
                cells,
                lax.ppermute(head, axis, [((i + 1) % count, i) for i in range(ends)]),
            ],
            axis=dim,
        )
    return cells


def from_partner(block, axis, bit):
    count = lax.axis_size(axis)
    route = []
    for low in range(count):
        high = low | 1 << bit
        if high != low and high < count:
            route += [(low, high), (high, low)]
    return lax.ppermute(block, axis, route)


def factor_solve(matrix, right):
    factor = lax.linalg.cholesky(matrix)
    forward = lax.linalg.triangular_solve(factor, right, left_side=True, lower=True)
    return lax.linalg.triangular_solve(
        factor, forward, left_side=True, lower=True, transpose_a=True
    )


def invert_blocks(matrices):
    identity = jnp.broadcast_to(jnp.eye(matrices.shape[-1], dtype=matrices.dtype), matrices.shape)
    return factor_solve(matrices, identity)


def beside_all(padded):
    return padded[2:, 1:-1] + padded[:-2, 1:-1] + padded[1:-1, 2:] + padded[1:-1, :-2]


def block_apply(inverse, field):
    if field.ndim == 4:
        return jnp.einsum("tsij,tsjc->tsic", inverse, field, precision=HIGH)
    return jnp.einsum("tsij,tsj->tsi", inverse, field, precision=HIGH)


def body(
    coupling,
    leaf_rhs,
    conductance,
    compressor,
    blocks,
    parent_of,
    parent_mat,
    parent_rhs,
    link,
    root_mat,
    root_rhs,
):
    dense = coupling[0].astype(jnp.float32)
    right = leaf_rhs[0]
    weight = conductance[0] * (1.0 + compressor[0].astype(jnp.float32)[..., None]) * 0.5
    column_weight = weight[..., None]
    own_blocks = blocks[0]
    inverse = invert_blocks(own_blocks)
    powers = [block_apply(inverse, dense)]
    vectors = [block_apply(inverse, right)]
    for sweep_index in range(ITERS // 2):
        outer, outer_vector = (
            extended(powers[-1] * column_weight, (("space", 1), ("tm", 0)), 1),
            extended(vectors[-1] * weight, (("space", 1), ("tm", 0)), 1),
        )
        powers.append(block_apply(inverse, beside_all(outer) * column_weight))
        vectors.append(block_apply(inverse, beside_all(outer_vector) * weight))
    schur = jnp.einsum("tsic,tsid->cd", dense, powers[0] + powers[1], precision=HIGH)
    gather_term = jnp.einsum("tsic,tsi->c", dense, vectors[0] + vectors[1], precision=HIGH)
    for power_index in range(1, ITERS // 2):
        lifted = block_apply(own_blocks, powers[power_index])
        schur = schur + jnp.einsum(
            "tsic,tsid->cd", lifted, powers[power_index] + powers[power_index + 1], precision=HIGH
        )
        gather_term = gather_term + jnp.einsum(
            "tsic,tsi->c", lifted, vectors[power_index] + vectors[power_index + 1], precision=HIGH
        )
    strip, gather_strip = (
        lax.psum_scatter(schur, ("space", "tm"), scatter_dimension=0, tiled=True),
        lax.psum_scatter(gather_term, ("space", "tm"), scatter_dimension=0, tiled=True),
    )
    parent_label = parent_of[0]
    parent_slots = (jnp.arange(PARENTS, dtype=jnp.int32) == parent_label).astype(jnp.float32)
    group = lax.axis_size("scen") // PARENTS
    for bit_index in range(group.bit_length() - 1):
        partner, partner_vector = from_partner((strip, gather_strip), "scen", bit_index)
        strip = strip + partner
        gather_strip = gather_strip + partner_vector
    hess_strip = jnp.einsum("p,pij->ij", parent_slots, parent_mat, precision=HIGH) + strip
    right_strip = gather_strip - jnp.einsum("p,pi->i", parent_slots, parent_rhs, precision=HIGH)
    link_strip = jnp.einsum("p,pin->in", parent_slots, link, precision=HIGH)
    hessian, reduced, own_link = (
        lax.all_gather(hess_strip, ("space", "tm"), axis=0, tiled=True),
        lax.all_gather(right_strip, ("space", "tm"), axis=0, tiled=True),
        lax.all_gather(link_strip, ("space", "tm"), axis=0, tiled=True),
    )
    link_solved = factor_solve(hessian, own_link)
    vector_solved = factor_solve(hessian, reduced[:, None])[:, 0]
    leader = (lax.axis_index("scen") % group == 0).astype(jnp.float32)
    root_term, right_term = lax.psum(
        (
            jnp.einsum("in,im->nm", own_link, link_solved, precision=HIGH) * leader,
            jnp.einsum("in,i->n", own_link, vector_solved, precision=HIGH) * leader,
        ),
        "scen",
    )
    root_step = factor_solve(root_mat + root_term, (root_rhs - right_term)[:, None])[:, 0]
    parent_step = vector_solved + jnp.einsum("in,n->i", link_solved, root_step, precision=HIGH)
    share_rows = parent_step.shape[0] // (lax.axis_size("space") * lax.axis_size("tm"))
    strip_index = lax.axis_index("space") * lax.axis_size("tm") + lax.axis_index("tm")
    parent_at_leaf = lax.dynamic_slice_in_dim(parent_step, strip_index * share_rows, share_rows)[
        None
    ]
    source = right - jnp.einsum("tsic,c->tsi", dense, parent_step, precision=HIGH)
    leaf_move = block_apply(inverse, source)
    for sweep_index in range(ITERS - 1):
        outer_vector = extended(leaf_move * weight, (("space", 1), ("tm", 0)), 1)
        leaf_move = block_apply(inverse, source + beside_all(outer_vector) * weight)
    return (leaf_move[None], parent_at_leaf, root_step)


def solution(mesh):
    return jax.shard_map(
        body,
        mesh=mesh,
        in_specs=(
            P("scen", "tm", "space", None, None),
            P("scen", "tm", "space", None),
            P("scen", "tm", "space", None),
            P("scen", "tm", "space"),
            P("scen", "tm", "space", None, None),
            P("scen"),
            P(None, ("space", "tm"), None),
            P(None, ("space", "tm")),
            P(None, ("space", "tm"), None),
            P(),
            P(),
        ),
        out_specs=(P("scen", "tm", "space", None), P("scen", ("space", "tm")), P()),
        check_vma=False,
    )
```

profile of v0, /device:TPU:0, one launch (start us, length us, event | category | flops | bytes accessed | tf_op | source)
XLA Modules:
  0.0 686.6 jit_solution(5895332855799410368)
XLA Ops:
  8.6 23.5 %custom-call.49 = f32[2,1,128,128]{3,2,1,0:T(8,128)S(1)} custom-call(f32[2,1,128,128]{3,2,1,0:T(8,128)S(1)} %fusion.95), custom_call_target="Cholesky" | custom-call | tf_op jit(solution)/shard_map/cholesky | solution.py:41
  32.3 19.7 %custom-call.50 = f32[2,1,1,128,128]{3,4,2,1,0:T(8,128)S(1)} custom-call(f32[2,1,1,128,128]{4,3,2,1,0:T(8,128)S(1)} %fusion.105), custom_call_target="InvertDiagBlocksLowerTriangular" | custom-call | tf_op jit(solution)/shard_map/triangular_solve | solution.py:43
  61.0 9.9 %collective-permute-done = f32[2,1,128,512]{3,2,0,1:T(8,128)S(1)} collective-permute-done((f32[2,1,128,512]{3,2,0,1:T(8,128)S(1)}, f32[2,1,128,512]{3,2,0,1:T(8,128)S(1)}, u32[]{:S(2)}, u32[]{:S(2)}) %collective-permute-start) | collective-permute-done | bytes 524320 | tf_op jit(solution)/shard_map/ppermute | solution.py:21
  70.9 16.2 %collective-permute-done.1 = f32[2,1,128,512]{3,2,0,1:T(8,128)S(1)} collective-permute-done((f32[2,1,128,512]{3,2,0,1:T(8,128)S(1)}, f32[2,1,128,512]{3,2,0,1:T(8,128)S(1)}, u32[]{:S(2)}, u32[]{:S(2)}) %collective-permute-start.1) | collective-permute-done | bytes 524320 | tf_op jit(solution)/shard_map/ppermute | solution.py:23
  90.1 14.8 %collective-permute-done.3 = f32[1,3,128,512]{3,2,0,1:T(8,128)S(1)} collective-permute-done((f32[1,3,128,512]{3,2,0,1:T(8,128)S(1)}, f32[1,3,128,512]{3,2,0,1:T(8,128)S(1)}, u32[]{:S(2)}, u32[]{:S(2)}) %collective-permute-start.3) | collective-permute-done | bytes 786464 | tf_op jit(solution)/shard_map/ppermute | solution.py:21
  123.3 15.2 %collective-permute-done.5 = f32[2,1,128,512]{3,2,0,1:T(8,128)S(1)} collective-permute-done((f32[2,1,128,512]{3,2,0,1:T(8,128)S(1)}, f32[2,1,128,512]{3,2,0,1:T(8,128)S(1)}, u32[]{:S(2)}, u32[]{:S(2)}) %collective-permute-start.5) | collective-permute-done | bytes 524320 | tf_op jit(solution)/shard_map/ppermute | solution.py:23
  174.5 15.2 %collective-permute-done.9 = f32[2,1,128,512]{3,2,0,1:T(8,128)S(1)} collective-permute-done((f32[2,1,128,512]{3,2,0,1:T(8,128)S(1)}, f32[2,1,128,512]{3,2,0,1:T(8,128)S(1)}, u32[]{:S(2)}, u32[]{:S(2)}) %collective-permute-start.9) | collective-permute-done | bytes 524320 | tf_op jit(solution)/shard_map/ppermute | solution.py:23
  195.9 12.7 %collective-permute-done.11 = f32[1,3,128,512]{3,2,0,1:T(8,128)S(1)} collective-permute-done((f32[1,3,128,512]{3,2,0,1:T(8,128)S(1)}, f32[1,3,128,512]{3,2,0,1:T(8,128)S(1)}, u32[]{:S(2)}, u32[]{:S(2)}) %collective-permute-start.11) | collective-permute-done | bytes 786464 | tf_op jit(solution)/shard_map/ppermute | solution.py:21
  219.5 22.9 %all_gather.11 = f32[512,256]{1,0:T(8,128)S(1)} all-gather(f32[128,256]{1,0:T(8,128)} %bitcast.492), channel_id=1, replica_groups=mesh['scen'=8,'space'=2,'tm'=2] {'space','tm'}, dimensions={0}, use_global_device_ids=true | all-gather | bytes 655360 | tf_op jit(solution)/shard_map/all_gather | solution.py:118
  276.3 12.7 %all-reduce.2 = f32[512]{0:T(512)S(1)} all-reduce(f32[512]{0:T(512)S(1)} %add_add_fusion), channel_id=3, replica_groups=mesh['scen'=8,'space'=2,'tm'=2] {'space','tm'}, use_global_device_ids=true, to_apply=%region_11.14.clone | all-reduce | flops 512 | bytes 4096
  310.2 11.7 %custom-call.55 = f32[128,128]{1,0:T(8,128)S(1)} custom-call(f32[128,128]{1,0:T(8,128)S(1)} %slice.443), custom_call_target="Cholesky" | custom-call | tf_op jit(solution)/shard_map/cholesky/custom-call.4 | solution.py:41
  322.0 9.8 %custom-call.56 = f32[1,128,128]{1,2,0:T(8,128)S(1)} custom-call(f32[1,128,128]{2,1,0:T(8,128)S(1)} %get-tuple-element.64), custom_call_target="InvertDiagBlocksLowerTriangular" | custom-call | tf_op jit(solution)/shard_map/cholesky/custom-call.18 | solution.py:41
  336.0 12.6 %custom-call.57 = f32[128,128]{1,0:T(8,128)S(1)} custom-call(f32[128,128]{1,0:T(8,128)} %slice.447), custom_call_target="Cholesky" | custom-call | tf_op jit(solution)/shard_map/cholesky/custom-call.5 | solution.py:41
  351.0 10.0 %custom-call.58 = f32[1,128,128]{1,2,0:T(8,128)S(1)} custom-call(f32[1,128,128]{2,1,0:T(8,128)S(1)} %get-tuple-element.61), custom_call_target="InvertDiagBlocksLowerTriangular" | custom-call | tf_op jit(solution)/shard_map/cholesky/custom-call.19 | solution.py:41
  363.4 11.7 %custom-call.59 = f32[128,128]{1,0:T(8,128)S(1)} custom-call(f32[128,128]{1,0:T(8,128)S(1)} %slice.452), custom_call_target="Cholesky" | custom-call | tf_op jit(solution)/shard_map/cholesky/custom-call.6 | solution.py:41
  387.8 11.9 %custom-call.61 = f32[128,128]{1,0:T(8,128)S(1)} custom-call(f32[128,128]{1,0:T(8,128)S(1)} %convolution_subtract_fusion.9), custom_call_target="Cholesky" | custom-call | tf_op jit(solution)/shard_map/cholesky/custom-call.7 | solution.py:41
  407.3 14.0 %while.2 = (s32[]{:T(128)}, f32[512,512]{1,0:T(8,128)}, s32[4,2]{0,1:T(2,128)S(1)}, f32[4,128,128]{2,1,0:T(8,128)}, s32[]{:T(128)}) while((s32[]{:T(128)}, f32[512,512]{1,0:T(8,128)}, s32[4,2]{0,1:T(2,128)S(1)}, f32[4,128,128]{2,1,0:T(8,128)}, s32[]{:T(128)}) %tuple.64), condition=%wide.while_cond, body=%wide.while_body.sunk | while | flops 2 | bytes 132205 | solution.py:43
  421.3 40.1 %custom-call.51 = f32[4,128,128]{1,2,0:T(8,128)S(1)} custom-call(f32[4,128,128]{2,1,0:T(8,128)} %get-tuple-element.12), custom_call_target="InvertDiagBlocksLowerTriangular" | custom-call | tf_op jit(solution)/shard_map/triangular_solve | solution.py:43
  477.7 12.6 %psum.15 = f32[256]{0:T(256)S(1)} all-reduce(f32[256]{0:T(256)S(1)} %bitcast.527), channel_id=1, replica_groups=mesh['scen'=8,'space'=2,'tm'=2] {'scen'}, use_global_device_ids=true, to_apply=%region_17.20 | all-reduce | flops 256 | bytes 2048 | tf_op jit(solution)/shard_map/psum | solution.py:123
  492.8 34.9 %all-reduce.5.cloned.1.call-done = f32[256,256]{0,1:T(8,128)} async-done(((f32[256,256]{0,1:T(8,128)}), f32[256,256]{0,1:T(8,128)}) %all-reduce.5.cloned.1.call-update) | async-done | bytes 262160 | tf_op jit(solution)/shard_map/psum | solution.py:123
  529.6 11.7 %cholesky.104 = f32[128,128]{1,0:T(8,128)S(1)} custom-call(f32[128,128]{1,0:T(8,128)S(1)} %cholesky.127), custom_call_target="Cholesky" | custom-call | tf_op jit(solution)/shard_map/cholesky | solution.py:41
  541.4 9.8 %custom-call.62 = f32[1,128,128]{1,2,0:T(8,128)S(1)} custom-call(f32[1,128,128]{2,1,0:T(8,128)S(1)} %get-tuple-element.54), custom_call_target="InvertDiagBlocksLowerTriangular" | custom-call | tf_op jit(solution)/shard_map/cholesky/custom-call.9 | solution.py:41
  553.4 11.7 %cholesky.114 = f32[128,128]{1,0:T(8,128)S(1)} custom-call(f32[128,128]{1,0:T(8,128)S(1)} %convolution_subtract_fusion.8), custom_call_target="Cholesky" | custom-call | tf_op jit(solution)/shard_map/cholesky | solution.py:41
  573.6 20.6 %custom-call.52 = f32[2,128,128]{1,2,0:T(8,128)S(1)} custom-call(f32[2,128,128]{2,1,0:T(8,128)} %get-tuple-element.20), custom_call_target="InvertDiagBlocksLowerTriangular" | custom-call | tf_op jit(solution)/shard_map/triangular_solve | solution.py:43
  (328 shorter events, 299.5 us)
Async XLA Ops:
  7.2 260.5 %reduce-scatter.2.cloned.1.call-start = ((), (), s32[]{:S(2)}) async-start(), calls=%async_computation.1 | async-start | bytes 1310720 | tf_op jit(solution)/shard_map/reduce_scatter | solution.py:102
  53.7 17.2 %collective-permute-start = (f32[2,1,128,512]{3,2,0,1:T(8,128)S(1)}, f32[2,1,128,512]{3,2,0,1:T(8,128)S(1)}, u32[]{:S(2)}, u32[]{:S(2)}) collective-permute-start(f32[2,1,128,512]{3,2,0,1:T(8,128)S(1)} %multiply_bitcast_fusion.2), channel_id=1, source_target_pairs={{0,2},{1,3},{4,6},{5,7},{8,10},{9,11},{12,14},{13,15},{16,18},{17,... | collective-permute-start | bytes 1572872 | tf_op jit(solution)/shard_map/ppermute | solution.py:21
  59.7 27.4 %collective-permute-start.1 = (f32[2,1,128,512]{3,2,0,1:T(8,128)S(1)}, f32[2,1,128,512]{3,2,0,1:T(8,128)S(1)}, u32[]{:S(2)}, u32[]{:S(2)}) collective-permute-start(f32[2,1,128,512]{3,2,0,1:T(8,128)S(1)} %multiply_bitcast_fusion.2), channel_id=1, source_target_pairs={{2,0},{3,1},{6,4},{7,5},{10,8},{11,9},{14,12},{15,13},{18,16},{19,... | collective-permute-start | bytes 1572872 | tf_op jit(solution)/shard_map/ppermute | solution.py:23
  87.5 17.5 %collective-permute-start.3 = (f32[1,3,128,512]{3,2,0,1:T(8,128)S(1)}, f32[1,3,128,512]{3,2,0,1:T(8,128)S(1)}, u32[]{:S(2)}, u32[]{:S(2)}) collective-permute-start(f32[1,3,128,512]{3,2,0,1:T(8,128)S(1)} %get-tuple-element.50), channel_id=1, source_target_pairs={{0,1},{2,3},{4,5},{6,7},{8,9},{10,11},{12,13},{14,15},{16,17},{18,... | collective-permute-start | bytes 2359304 | tf_op jit(solution)/shard_map/ppermute | solution.py:21
  88.8 20.3 %collective-permute-start.2 = (f32[1,3,128,512]{3,2,0,1:T(8,128)S(1)}, f32[1,3,128,512]{3,2,0,1:T(8,128)S(1)}, u32[]{:S(2)}, u32[]{:S(2)}) collective-permute-start(f32[1,3,128,512]{3,2,0,1:T(8,128)S(1)} %get-tuple-element.49), channel_id=1, source_target_pairs={{1,0},{3,2},{5,4},{7,6},{9,8},{11,10},{13,12},{15,14},{17,16},{19,... | collective-permute-start | bytes 2359304 | tf_op jit(solution)/shard_map/ppermute | solution.py:23
  109.9 13.3 %collective-permute-start.4 = (f32[2,1,128,512]{3,2,0,1:T(8,128)S(1)}, f32[2,1,128,512]{3,2,0,1:T(8,128)S(1)}, u32[]{:S(2)}, u32[]{:S(2)}) collective-permute-start(f32[2,1,128,512]{3,2,0,1:T(8,128)S(1)} %multiply_bitcast_fusion.1), channel_id=1, source_target_pairs={{0,2},{1,3},{4,6},{5,7},{8,10},{9,11},{12,14},{13,15},{16,18},{17,... | collective-permute-start | bytes 1572872 | tf_op jit(solution)/shard_map/ppermute | solution.py:21
  113.1 25.4 %collective-permute-start.5 = (f32[2,1,128,512]{3,2,0,1:T(8,128)S(1)}, f32[2,1,128,512]{3,2,0,1:T(8,128)S(1)}, u32[]{:S(2)}, u32[]{:S(2)}) collective-permute-start(f32[2,1,128,512]{3,2,0,1:T(8,128)S(1)} %multiply_bitcast_fusion.1), channel_id=1, source_target_pairs={{2,0},{3,1},{6,4},{7,5},{10,8},{11,9},{14,12},{15,13},{18,16},{19,... | collective-permute-start | bytes 1572872 | tf_op jit(solution)/shard_map/ppermute | solution.py:23
  138.8 18.6 %collective-permute-start.7 = (f32[1,3,128,512]{3,2,0,1:T(8,128)S(1)}, f32[1,3,128,512]{3,2,0,1:T(8,128)S(1)}, u32[]{:S(2)}, u32[]{:S(2)}) collective-permute-start(f32[1,3,128,512]{3,2,0,1:T(8,128)S(1)} %get-tuple-element.48), channel_id=1, source_target_pairs={{0,1},{2,3},{4,5},{6,7},{8,9},{10,11},{12,13},{14,15},{16,17},{18,... | collective-permute-start | bytes 2359304 | tf_op jit(solution)/shard_map/ppermute | solution.py:21
  140.1 21.4 %collective-permute-start.6 = (f32[1,3,128,512]{3,2,0,1:T(8,128)S(1)}, f32[1,3,128,512]{3,2,0,1:T(8,128)S(1)}, u32[]{:S(2)}, u32[]{:S(2)}) collective-permute-start(f32[1,3,128,512]{3,2,0,1:T(8,128)S(1)} %get-tuple-element.47), channel_id=1, source_target_pairs={{1,0},{3,2},{5,4},{7,6},{9,8},{11,10},{13,12},{15,14},{17,16},{19,... | collective-permute-start | bytes 2359304 | tf_op jit(solution)/shard_map/ppermute | solution.py:23
  141.4 25.5 %collective-permute-start.12 = (f32[2,1,128]{2,0,1:T(2,128)S(1)}, f32[2,1,128]{2,0,1:T(2,128)S(1)}, u32[]{:S(2)}, u32[]{:S(2)}) collective-permute-start(f32[2,1,128]{2,0,1:T(2,128)S(1)} %get-tuple-element.39), channel_id=1, source_target_pairs={{0,2},{1,3},{4,6},{5,7},{8,10},{9,11},{12,14},{13,15},{16,18},{17,... | collective-permute-start | bytes 3080 | tf_op jit(solution)/shard_map/ppermute | solution.py:21
  142.9 24.1 %collective-permute-start.13 = (f32[2,1,128]{2,0,1:T(2,128)S(1)}, f32[2,1,128]{2,0,1:T(2,128)S(1)}, u32[]{:S(2)}, u32[]{:S(2)}) collective-permute-start(f32[2,1,128]{2,0,1:T(2,128)S(1)} %get-tuple-element.39), channel_id=1, source_target_pairs={{2,0},{3,1},{6,4},{7,5},{10,8},{11,9},{14,12},{15,13},{18,16},{19,... | collective-permute-start | bytes 3080 | tf_op jit(solution)/shard_map/ppermute | solution.py:23
  162.3 12.1 %collective-permute-start.8 = (f32[2,1,128,512]{3,2,0,1:T(8,128)S(1)}, f32[2,1,128,512]{3,2,0,1:T(8,128)S(1)}, u32[]{:S(2)}, u32[]{:S(2)}) collective-permute-start(f32[2,1,128,512]{3,2,0,1:T(8,128)S(1)} %multiply_bitcast_fusion), channel_id=1, source_target_pairs={{0,2},{1,3},{4,6},{5,7},{8,10},{9,11},{12,14},{13,15},{16,18},{17,... | collective-permute-start | bytes 1572872 | tf_op jit(solution)/shard_map/ppermute | solution.py:21
  163.8 25.9 %collective-permute-start.9 = (f32[2,1,128,512]{3,2,0,1:T(8,128)S(1)}, f32[2,1,128,512]{3,2,0,1:T(8,128)S(1)}, u32[]{:S(2)}, u32[]{:S(2)}) collective-permute-start(f32[2,1,128,512]{3,2,0,1:T(8,128)S(1)} %multiply_bitcast_fusion), channel_id=1, source_target_pairs={{2,0},{3,1},{6,4},{7,5},{10,8},{11,9},{14,12},{15,13},{18,16},{19,... | collective-permute-start | bytes 1572872 | tf_op jit(solution)/shard_map/ppermute | solution.py:23
  167.0 25.7 %collective-permute-start.15 = (f32[1,3,128]{2,0,1:T(1,128)S(1)}, f32[1,3,128]{2,0,1:T(1,128)S(1)}, u32[]{:S(2)}, u32[]{:S(2)}) collective-permute-start(f32[1,3,128]{2,0,1:T(1,128)S(1)} %get-tuple-element.80), channel_id=1, source_target_pairs={{0,1},{2,3},{4,5},{6,7},{8,9},{10,11},{12,13},{14,15},{16,17},{18,... | collective-permute-start | bytes 4616 | tf_op jit(solution)/shard_map/ppermute | solution.py:21
  168.4 24.3 %collective-permute-start.14 = (f32[1,3,128]{2,0,1:T(1,128)S(1)}, f32[1,3,128]{2,0,1:T(1,128)S(1)}, u32[]{:S(2)}, u32[]{:S(2)}) collective-permute-start(f32[1,3,128]{2,0,1:T(1,128)S(1)} %get-tuple-element.79), channel_id=1, source_target_pairs={{1,0},{3,2},{5,4},{7,6},{9,8},{11,10},{13,12},{15,14},{17,16},{19,... | collective-permute-start | bytes 4616 | tf_op jit(solution)/shard_map/ppermute | solution.py:23
  190.1 18.5 %collective-permute-start.11 = (f32[1,3,128,512]{3,2,0,1:T(8,128)S(1)}, f32[1,3,128,512]{3,2,0,1:T(8,128)S(1)}, u32[]{:S(2)}, u32[]{:S(2)}) collective-permute-start(f32[1,3,128,512]{3,2,0,1:T(8,128)S(1)} %get-tuple-element.46), channel_id=1, source_target_pairs={{0,1},{2,3},{4,5},{6,7},{8,9},{10,11},{12,13},{14,15},{16,17},{18,... | collective-permute-start | bytes 2359304 | tf_op jit(solution)/shard_map/ppermute | solution.py:21
  191.4 21.4 %collective-permute-start.10 = (f32[1,3,128,512]{3,2,0,1:T(8,128)S(1)}, f32[1,3,128,512]{3,2,0,1:T(8,128)S(1)}, u32[]{:S(2)}, u32[]{:S(2)}) collective-permute-start(f32[1,3,128,512]{3,2,0,1:T(8,128)S(1)} %get-tuple-element.45), channel_id=1, source_target_pairs={{1,0},{3,2},{5,4},{7,6},{9,8},{11,10},{13,12},{15,14},{17,16},{19,... | collective-permute-start | bytes 2359304 | tf_op jit(solution)/shard_map/ppermute | solution.py:23
  216.4 88.5 %all-gather.3.cloned.1.call-start = ((), (), s32[]{:S(2)}) async-start(), calls=%async_computation.2 | async-start | bytes 1310720 | tf_op jit(solution)/shard_map/all_gather | solution.py:116
  216.7 25.7 %collective-permute-start.16 = (f32[2,1,128]{2,0,1:T(2,128)S(1)}, f32[2,1,128]{2,0,1:T(2,128)S(1)}, u32[]{:S(2)}, u32[]{:S(2)}) collective-permute-start(f32[2,1,128]{2,0,1:T(2,128)S(1)} %multiply_bitcast_fusion.9), channel_id=1, source_target_pairs={{0,2},{1,3},{4,6},{5,7},{8,10},{9,11},{12,14},{13,15},{16,18},{17,... | collective-permute-start | bytes 3080 | tf_op jit(solution)/shard_map/ppermute | solution.py:21
  218.2 24.2 %collective-permute-start.17 = (f32[2,1,128]{2,0,1:T(2,128)S(1)}, f32[2,1,128]{2,0,1:T(2,128)S(1)}, u32[]{:S(2)}, u32[]{:S(2)}) collective-permute-start(f32[2,1,128]{2,0,1:T(2,128)S(1)} %multiply_bitcast_fusion.9), channel_id=1, source_target_pairs={{2,0},{3,1},{6,4},{7,5},{10,8},{11,9},{14,12},{15,13},{18,16},{19,... | collective-permute-start | bytes 3080 | tf_op jit(solution)/shard_map/ppermute | solution.py:23
  250.6 12.2 %collective-permute-start.20 = (f32[2,1,128]{2,0,1:T(2,128)}, f32[2,1,128]{2,0,1:T(2,128)}, u32[]{:S(2)}, u32[]{:S(2)}) collective-permute-start(f32[2,1,128]{2,0,1:T(2,128)} %multiply_bitcast_fusion.8), channel_id=1, source_target_pairs={{0,2},{1,3},{4,6},{5,7},{8,10},{9,11},{12,14},{13,15},{16,18},{17,... | collective-permute-start | bytes 3080 | tf_op jit(solution)/shard_map/ppermute | solution.py:21
  255.7 7.2 %collective-permute-start.21 = (f32[2,1,128]{2,0,1:T(2,128)}, f32[2,1,128]{2,0,1:T(2,128)}, u32[]{:S(2)}, u32[]{:S(2)}) collective-permute-start(f32[2,1,128]{2,0,1:T(2,128)} %multiply_bitcast_fusion.8), channel_id=1, source_target_pairs={{2,0},{3,1},{6,4},{7,5},{10,8},{11,9},{14,12},{15,13},{18,16},{19,... | collective-permute-start | bytes 3080 | tf_op jit(solution)/shard_map/ppermute | solution.py:23
  269.5 258.2 %all-reduce.5.cloned.1.call-start = ((), (), s32[]{:S(2)}) async-start(), calls=%async_computation.3 | async-start | bytes 524288 | tf_op jit(solution)/shard_map/psum | solution.py:123
  601.7 6.4 collective-permute-start.25
  (47 other events, 890.9 us)
Sparse Core Ops, SparseCore 0:
  216.5 33.5 reduce-scatter.1
  269.6 35.2 all-gather.2
  476.8 50.8 all-reduce.4
where the time goes:
time: 696 us; the launch traced here: 687 us
  other arithmetic  236 us (34%)
  waiting for transfers between devices  213 us (31%)
  starting transfers between devices  77.7 us (11%)
  blocking collectives  56.2 us (8%)
  matrix products  47.4 us (7%)
  local copies, waits for them, and re-layouts  36.2 us (5%)
  between operations  20.3 us (3%)
    another operation x25, other arithmetic, factor_solve(): factor = lax.linalg.cholesky(matrix)  140 us
    ppermute x22, waiting for transfers between devices, extended(): lax.ppermute(head, axis, [((i + 1) % count, i) for i in range(ends)])  110 us
    another operation x11, other arithmetic, factor_solve(): lax.linalg.triangular_solve(factor, forward, left_side=True, lower=True,...  85.8 us
    ppermute x22, waiting for transfers between devices, extended(): lax.ppermute(tail, axis, [(i, (i + 1) % count) for i in range(ends)])  60.5 us
    ppermute x22, starting transfers between devices, extended(): lax.ppermute(tail, axis, [(i, (i + 1) % count) for i in range(ends)])  49 us
    psum x1, waiting for transfers between devices, body(): lax.psum((jnp.einsum('in,im->nm', own_link, link_solved, precision=HIGH)...  34.9 us
    ppermute x22, starting transfers between devices, extended(): lax.ppermute(head, axis, [((i + 1) % count, i) for i in range(ends)])  28.6 us
    all_gather x1, blocking collectives, body(): lax.all_gather(link_strip, ('space', 'tm'), axis=0, tiled=True)  22.9 us
  transfers between devices with their start and end apart: 47, of which 26 were waited for; matrix products, arithmetic and copies ran while one was open for 4% of the time, Pallas kernels for 0%

commit v1 on v0

v1 whole, which is shorter than its diff:
```python
import functools

import jax
import jax.numpy as jnp
from jax import lax
from jax.experimental import pallas as pl
from jax.experimental.pallas import tpu as pltpu
from jax.sharding import PartitionSpec as P

PARENTS = 8
ITERS = 6
LANES = 128
F32 = jnp.float32
BF16 = jnp.bfloat16
HIGH = lax.Precision.HIGHEST
MESH = pl.DeviceIdType.MESH
VMEM = pl.BlockSpec(memory_space=pltpu.VMEM)
ANY = pl.BlockSpec(memory_space=pl.ANY)
LIMIT = 56 * 1024 * 1024
SETTLED = 1e-7
NN = ((1,), (0,))
NT = ((1,), (1,))
TN = ((0,), (0,))


def full_dot(a, b, dims=NN):
    return lax.dot_general(a, b, (dims, ((), ())), precision=HIGH, preferred_element_type=F32)


def fast_dot(a, b, dims=NN):
    return lax.dot_general(a, b, (dims, ((), ())), preferred_element_type=F32)


def halves(x):
    top = x.astype(BF16)
    return top, (x - top.astype(F32)).astype(BF16)


def as_columns(row):
    return jnp.broadcast_to(row, (LANES, LANES)).T


def spd_inverses(matrices):
    size = matrices[0].shape[0]
    row = lax.broadcasted_iota(jnp.int32, (size, size), 0)
    column = lax.broadcasted_iota(jnp.int32, (size, size), 1)
    identity = jnp.where(row == column, 1.0, 0.0).astype(F32)
    rho = None
    pairs = []
    for matrix in matrices:
        square = full_dot(matrix, matrix)
        plain = jnp.max(jnp.sum(jnp.abs(matrix), axis=0, keepdims=True), axis=1, keepdims=True)
        squared = jnp.max(jnp.sum(jnp.abs(square), axis=0, keepdims=True), axis=1, keepdims=True)
        bound = jnp.maximum(jnp.minimum(plain, jnp.sqrt(squared)) * 1.0001, 1.0)
        total, spread = bound + 1.0, bound - 1.0
        scale = 1.0 / (2.0 * total * total - spread * spread)
        alpha, beta = 8.0 * total * scale, 8.0 * scale
        start = alpha * identity - beta * matrix
        residual = identity - alpha * matrix + beta * square
        pairs.append((start, residual))
        own = jnp.max(spread * spread * scale)
        rho = own if rho is None else jnp.maximum(rho, own)

    def more(state):
        return (state[0] > SETTLED) & (state[1] < 32)

    def step(state):
        norm, count, items = state
        after = []
        for x, r in items:
            both = full_dot(jnp.concatenate([x, r], axis=0), r)
            after.append((x + both[:size], both[size:]))
        return norm * norm, count + 1, after

    return [x for x, _ in lax.while_loop(more, step, (rho, jnp.int32(0), pairs))[2]]


def block_kernel(blocks_ref, inverse_ref):
    count, size, _ = blocks_ref.shape
    zero = jnp.zeros((size, size), F32)
    for i in range(0, count, 2):
        j = min(i + 1, count - 1)
        pair = jnp.concatenate(
            [
                jnp.concatenate([blocks_ref[i], zero], axis=1),
                jnp.concatenate([zero, blocks_ref[j]], axis=1),
            ],
            axis=0,
        )
        found = spd_inverses([pair])[0]
        inverse_ref[i] = found[:size, :size]
        inverse_ref[j] = found[size:, size:]


def leaf_kernel(beside, per, coupling_ref, inverse_ref, vector_ref, schur_ref, solved_ref,
                field, plain, scaled, weight_ref, bits):
    count = len(beside)
    columns = coupling_ref.shape[-1]
    wide = columns + LANES

    def stacked(matrix):
        top, low = halves(matrix)
        return jnp.concatenate([top, low, top], axis=1)

    def stack(x):
        top, low = halves(x)
        return jnp.concatenate([top, top, low], axis=0)

    def source(n, start, width):
        g, k = divmod(n, per)
        parts = []
        if start < columns:
            parts.append(coupling_ref[g, k, :, pl.ds(start, min(width, columns - start))])
        if start + width > columns:
            parts.append(as_columns(vector_ref[g, k:k + 1, :]))
        return jnp.concatenate(parts, axis=1)

    for n in range(count):
        g, k = divmod(n, per)
        weight_row = vector_ref[g, per + k:per + k + 1, :]
        weight = as_columns(weight_row)
        inverse = inverse_ref[g, k]
        weight_ref[n] = weight
        plain[n] = stacked(inverse)
        scaled[n] = stacked(weight * inverse * weight_row)
        bits[pl.ds(n * LANES, LANES), :] = coupling_ref[g, k].astype(BF16)

    def around(slot, n):
        total = field[slot, beside[n][0]]
        for m in beside[n][1:]:
            total = total + field[slot, m]
        return total

    width = field.shape[-1]
    last = (ITERS - 2) % 2
    for start in range(0, wide, width):
        here = pl.ds(start, width)

        def spread(n):
            return jnp.concatenate([weight_ref[n]] * (width // LANES), axis=1)

        for n in range(count):
            first = spread(n) * fast_dot(plain[n], stack(source(n, start, width)))
            field[0, n] = first
            solved_ref[n, :, here] = first

        def sweep(k, carry):
            now = lax.rem(k, 2)
            for n in range(count):
                moved = fast_dot(scaled[n], stack(around(now, n)))
                field[1 - now, n] = solved_ref[n, :, here] + moved
            return carry

        lax.fori_loop(0, ITERS - 2, sweep, 0)
        for n in range(count):
            drive = source(n, start, width) + spread(n) * around(last, n)
            solved_ref[n, :, here] = fast_dot(plain[n], stack(drive))
    chunk = min(count, 8)
    for c in range(0, count, chunk):
        top, low = halves(solved_ref[pl.ds(c, chunk)].reshape(chunk * LANES, wide))
        own = bits[pl.ds(c * LANES, chunk * LANES), :]
        part = fast_dot(own, top, TN) + fast_dot(own, low, TN)
        schur_ref[...] = part if c == 0 else schur_ref[...] + part


def parent_kernel(schur_ref, matrix_ref, right_ref, link_ref, solution_ref, term_ref):
    size = matrix_ref.shape[0]
    half = size // 2
    roots = link_ref.shape[1]
    wide = roots + LANES
    right = jnp.concatenate(
        [as_columns(right_ref[:, pl.ds(c, LANES)]) for c in range(0, size, LANES)], axis=0
    )
    sides = jnp.concatenate([link_ref[...], schur_ref[:, pl.ds(size, LANES)] - right], axis=1)
    a, b = pl.ds(0, half), pl.ds(half, half)
    h11 = matrix_ref[a, a] + schur_ref[a, a]
    h12 = matrix_ref[a, b] + schur_ref[a, b]
    h21 = matrix_ref[b, a] + schur_ref[b, a]
    h22 = matrix_ref[b, b] + schur_ref[b, b]
    x11 = spd_inverses([h11])[0]
    eliminated = full_dot(x11, jnp.concatenate([h12, sides[:half]], axis=1))
    rest = full_dot(h21, eliminated)
    x22 = spd_inverses([h22 - rest[:, :half]])[0]
    lower = full_dot(x22, sides[half:] - rest[:, half:])
    upper = eliminated[:, half:] - full_dot(eliminated[:, :half], lower)
    solution_ref[a, :] = upper
    solution_ref[b, :] = lower
    term_ref[...] = full_dot(solution_ref[...], link_ref[...], TN)[:roots + 8]


def root_kernel(matrix_ref, term_ref, vector_ref, right_ref, solution_ref, solved_ref, pack_ref):
    roots = matrix_ref.shape[0]
    size = solution_ref.shape[0]
    groups = pack_ref.shape[0]
    per = solved_ref.shape[0] // groups
    inverse = spd_inverses([matrix_ref[...] + term_ref[...]])[0]
    root = full_dot(right_ref[...] - vector_ref[...], inverse)
    lane = lax.broadcasted_iota(jnp.int32, (8, LANES), 1)
    unit = jnp.where(lane == 0, 1.0, 0.0).astype(F32)
    parent = full_dot(jnp.concatenate([root, unit], axis=1), solution_ref[...], NT)
    mix = jnp.concatenate([-parent, unit], axis=1)
    for g in range(groups):
        for k in range(per):
            pack_ref[g, :, pl.ds(k * LANES, LANES)] = full_dot(mix, solved_ref[g * per + k], NT)
        pack_ref[g, :, pl.ds(per * LANES, size)] = parent
        pack_ref[g, :, pl.ds(per * LANES + size, roots)] = root


class Plan:
    def __init__(self, mesh):
        self.scen, self.space, self.tm = (mesh.shape[name] for name in ("scen", "space", "tm"))
        self.members = self.space * self.tm
        self.siblings = self.scen // PARENTS

    def leader(self, scen):
        middle = self.members // 2
        if self.siblings == 1:
            return middle - lax.rem(scen, 2)
        return middle + 0 * scen

    def device(self, scen, member):
        return (scen, lax.div(member, self.tm), lax.rem(member, self.tm))

    def here(self):
        return lax.axis_index("scen"), lax.axis_index("space") * self.tm + lax.axis_index("tm")


def gather_kernel(plan, count, *refs):
    sources, targets = refs[:count], refs[count:2 * count]
    send, receive, local = refs[2 * count:]
    scen, member = plan.here()
    lead = plan.leader(scen)
    barrier = pltpu.get_barrier_semaphore()

    def remote(i, place, slot):
        return pltpu.make_async_remote_copy(
            src_ref=sources[i], dst_ref=targets[i].at[place], send_sem=send.at[i],
            recv_sem=receive.at[i, slot], device_id=plan.device(scen, lead), device_id_type=MESH,
        )

    @pl.when(member != lead)
    def _():
        pl.semaphore_signal(barrier, inc=1, device_id=plan.device(scen, lead), device_id_type=MESH)
        pl.semaphore_wait(barrier, 1)
        slot = lax.rem(member - lead + plan.members, plan.members) - 1
        copies = [remote(i, member, slot) for i in range(count)]
        for copy in copies:
            copy.start()
        for copy in copies:
            copy.wait_send()

    @pl.when(member == lead)
    def _():
        others = [lax.rem(lead + k, plan.members) for k in range(1, plan.members)]
        for other in others:
            pl.semaphore_signal(
                barrier, inc=1, device_id=plan.device(scen, other), device_id_type=MESH
            )
        own = [pltpu.make_async_copy(sources[i], targets[i].at[member], local.at[i]) for i in range(count)]
        for copy in own:
            copy.start()
        pl.semaphore_wait(barrier, plan.members - 1)
        for slot, other in enumerate(others):
            for i in range(count):
                remote(i, other, slot).wait_recv()
        for copy in own:
            copy.wait()


def gather(plan, arrays):
    count = len(arrays)
    return pl.pallas_call(
        functools.partial(gather_kernel, plan, count),
        out_shape=[jax.ShapeDtypeStruct((plan.members,) + x.shape, x.dtype) for x in arrays],
        in_specs=[ANY] * count,
        out_specs=[ANY] * count,
        scratch_shapes=[
            pltpu.SemaphoreType.DMA((count,)),
            pltpu.SemaphoreType.DMA((count, plan.members - 1)),
            pltpu.SemaphoreType.DMA((count,)),
        ],
        compiler_params=pltpu.CompilerParams(collective_id=0, has_side_effects=True),
    )(*arrays)


def sum_kernel(plan, term_ref, total_ref, vector_ref, strips, vectors, whole,
               send, receive):
    scen, member = plan.here()
    lead = plan.leader(scen)
    count = plan.scen
    roots = whole.shape[0]
    rows = roots // count
    barrier = pltpu.get_barrier_semaphore()

    @pl.when(member == lead)
    def _():
        peers = [lax.rem(scen + k, count) for k in range(1, count)]
        devices = [plan.device(peer, plan.leader(peer)) for peer in peers]
        for device in devices:
            pl.semaphore_signal(barrier, inc=1, device_id=device, device_id_type=MESH)
        mine = pl.ds(pl.multiple_of(scen * rows, rows), rows)
        strips[scen] = term_ref[mine, :]
        vectors[scen] = term_ref[pl.ds(roots, 8), :]
        pl.semaphore_wait(barrier, count - 1)

        def remote(kind, k, source, target):
            return pltpu.make_async_remote_copy(
                src_ref=source, dst_ref=target, send_sem=send.at[kind, k],
                recv_sem=receive.at[kind, k], device_id=devices[k], device_id_type=MESH,
            )

        copies = []
        for k, peer in enumerate(peers):
            theirs = pl.ds(pl.multiple_of(peer * rows, rows), rows)
            copies.append(remote(0, k, term_ref.at[theirs, :], strips.at[scen]))
            copies.append(remote(1, k, term_ref.at[pl.ds(roots, 8), :], vectors.at[scen]))
        for copy in copies:
            copy.start()
        for copy in copies:
            copy.wait()
        total = strips[0]
        vector = vectors[0]
        for s in range(1, count):
            total = total + strips[s]
            vector = vector + vectors[s]
        vector_ref[...] = vector
        whole[mine, :] = total
        copies = [remote(2, k, whole.at[mine, :], whole.at[mine, :]) for k in range(count - 1)]
        for copy in copies:
            copy.start()
        for copy in copies:
            copy.wait()
        total_ref[...] = whole[...]

    @pl.when(member != lead)
    def _():
        total_ref[...] = jnp.zeros_like(total_ref)
        vector_ref[...] = jnp.zeros_like(vector_ref)


def sum_terms(plan, term):
    roots = term.shape[1]
    return pl.pallas_call(
        functools.partial(sum_kernel, plan),
        out_shape=[jax.ShapeDtypeStruct((roots, roots), F32), jax.ShapeDtypeStruct((8, roots), F32)],
        in_specs=[VMEM],
        out_specs=[VMEM] * 2,
        scratch_shapes=[
            pltpu.VMEM((plan.scen, roots // plan.scen, roots), F32),
            pltpu.VMEM((plan.scen, 8, roots), F32),
            pltpu.VMEM((roots, roots), F32),
            pltpu.SemaphoreType.DMA((3, plan.scen - 1)),
            pltpu.SemaphoreType.DMA((3, plan.scen - 1)),
        ],
        compiler_params=pltpu.CompilerParams(collective_id=1, has_side_effects=True),
    )(term)


def scatter_kernel(plan, pack_ref, out_ref, landed, send, receive):
    scen, member = plan.here()
    lead = plan.leader(scen)
    barrier = pltpu.get_barrier_semaphore()

    def remote(k, other):
        return pltpu.make_async_remote_copy(
            src_ref=pack_ref.at[other], dst_ref=landed, send_sem=send.at[k],
            recv_sem=receive, device_id=plan.device(scen, other), device_id_type=MESH,
        )

    @pl.when(member != lead)
    def _():
        pl.semaphore_signal(barrier, inc=1, device_id=plan.device(scen, lead), device_id_type=MESH)
        pl.semaphore_wait(barrier, 1)
        remote(0, lead).wait_recv()
        out_ref[...] = landed[...]

    @pl.when(member == lead)
    def _():
        others = [lax.rem(lead + k, plan.members) for k in range(1, plan.members)]
        for other in others:
            pl.semaphore_signal(
                barrier, inc=1, device_id=plan.device(scen, other), device_id_type=MESH
            )
        pl.semaphore_wait(barrier, plan.members - 1)
        copies = [remote(k, other) for k, other in enumerate(others)]
        for copy in copies:
            copy.start()
        out_ref[...] = pack_ref[member]
        for copy in copies:
            copy.wait_send()


def scatter(plan, pack):
    return pl.pallas_call(
        functools.partial(scatter_kernel, plan),
        out_shape=jax.ShapeDtypeStruct(pack.shape[1:], F32),
        in_specs=[VMEM],
        out_specs=VMEM,
        scratch_shapes=[
            pltpu.VMEM(pack.shape[1:], F32),
            pltpu.SemaphoreType.DMA((plan.members - 1,)),
            pltpu.SemaphoreType.DMA,
        ],
        compiler_params=pltpu.CompilerParams(collective_id=2, has_side_effects=True),
    )(pack)


def local_call(kernel, out_shape, count, scratch=()):
    many = isinstance(out_shape, list)
    return pl.pallas_call(
        kernel,
        out_shape=out_shape,
        in_specs=[VMEM] * count,
        out_specs=[VMEM] * len(out_shape) if many else VMEM,
        scratch_shapes=list(scratch),
        compiler_params=pltpu.CompilerParams(vmem_limit_bytes=LIMIT),
    )


def from_partner(block, axis, bit):
    count = lax.axis_size(axis)
    route = []
    for low in range(count):
        high = low | 1 << bit
        if high != low and high < count:
            route += [(low, high), (high, low)]
    return lax.ppermute(block, axis, route)


def neighbours(plan, times, cells):
    place = {}
    for g in range(plan.members):
        for t in range(times):
            for s in range(cells):
                at = ((g % plan.tm) * times + t, (g // plan.tm) * cells + s)
                place[at] = (g * times + t) * cells + s
    found = [None] * len(place)
    for (t, s), n in place.items():
        sides = [(t + 1, s), (t - 1, s), (t, s + 1), (t, s - 1)]
        found[n] = [place[side] for side in sides if side in place]
    return found


def body(
    plan,
    coupling,
    leaf_rhs,
    conductance,
    compressor,
    blocks,
    parent_of,
    parent_mat,
    parent_rhs,
    link,
    root_mat,
    root_rhs,
):
    _, times, cells, rows, size = coupling.shape
    per = times * cells
    roots = root_rhs.shape[0]
    share = parent_rhs.shape[1]
    count = plan.members * per
    dense = coupling.reshape(per, rows, size).astype(F32)
    weight = conductance[0] * (1.0 + compressor[0].astype(F32)[..., None]) * 0.5
    inverse = local_call(block_kernel, jax.ShapeDtypeStruct((per, rows, rows), F32), 1)(
        blocks.reshape(per, rows, rows)
    )
    label = parent_of[0]
    own_mat = lax.dynamic_index_in_dim(parent_mat, label, 0, keepdims=False)
    own_rhs = lax.dynamic_index_in_dim(parent_rhs, label, 0, keepdims=True)
    own_link = lax.dynamic_index_in_dim(link, label, 0, keepdims=False)
    lines = jnp.concatenate(
        [
            leaf_rhs.reshape(per, rows),
            weight.reshape(per, rows),
            jnp.pad(own_rhs, ((0, 0), (0, LANES - share))),
        ],
        axis=0,
    )
    lines = jnp.pad(lines, ((0, -lines.shape[0] % 8), (0, 0)))
    all_dense, all_inverse, all_mat, all_link, all_lines = gather(
        plan, [dense, inverse, own_mat, own_link, lines]
    )
    wide = size + LANES
    schur, solved = local_call(
        functools.partial(leaf_kernel, neighbours(plan, times, cells), per),
        [jax.ShapeDtypeStruct((size, wide), F32), jax.ShapeDtypeStruct((count, rows, wide), F32)],
        3,
        [
            pltpu.VMEM((2, count, rows, wide if count <= 8 else LANES), F32),
            pltpu.VMEM((count, rows, 3 * rows), BF16),
            pltpu.VMEM((count, rows, 3 * rows), BF16),
            pltpu.VMEM((count, rows, LANES), F32),
            pltpu.VMEM((count * rows, size), BF16),
        ],
    )(all_dense, all_inverse, all_lines)
    for bit_index in range(plan.siblings.bit_length() - 1):
        schur = schur + from_partner(schur, "scen", bit_index)
    right = all_lines[:, 2 * per, :share].reshape(1, size)
    solution_p, term = local_call(
        parent_kernel,
        [
            jax.ShapeDtypeStruct((size, roots + LANES), F32),
            jax.ShapeDtypeStruct((roots + 8, roots), F32),
        ],
        4,
    )(schur, all_mat.reshape(size, size), right, all_link.reshape(size, roots))
    if plan.siblings > 1:
        term = jnp.where(lax.axis_index("scen") % plan.siblings == 0, term, 0.0)
    total, vector = sum_terms(plan, term)
    pack = local_call(
        root_kernel,
        jax.ShapeDtypeStruct((plan.members, 8, per * rows + size + roots), F32),
        6,
    )(root_mat, total, vector, root_rhs[None], solution_p, solved)
    line = scatter(plan, pack)[0]
    leaf_move = line[: per * rows].reshape(leaf_rhs.shape)
    strip = lax.axis_index("space") * plan.tm + lax.axis_index("tm")
    parent_at_leaf = lax.dynamic_slice_in_dim(line, per * rows + strip * share, share)[None]
    return leaf_move, parent_at_leaf, line[per * rows + size :]


def solution(mesh):
    return jax.shard_map(
        functools.partial(body, Plan(mesh)),
        mesh=mesh,
        in_specs=(
            P("scen", "tm", "space", None, None),
            P("scen", "tm", "space", None),
            P("scen", "tm", "space", None),
            P("scen", "tm", "space"),
            P("scen", "tm", "space", None, None),
            P("scen"),
            P(None, ("space", "tm"), None),
            P(None, ("space", "tm")),
            P(None, ("space", "tm"), None),
            P(),
            P(),
        ),
        out_specs=(P("scen", "tm", "space", None), P("scen", ("space", "tm")), P()),
        check_vma=False,
    )
```

time: 696 us -> 113 us (0.16); the launches traced: 687 us -> 112 us
  other arithmetic: 236 us -> 4.5 us
  waiting for transfers between devices: 213 us -> 0 us
  Pallas kernels: 0 us -> 98.9 us
  starting transfers between devices: 77.7 us -> 0 us
  blocking collectives: 56.2 us -> 0 us
  matrix products: 47.4 us -> 0 us
  local copies, waits for them, and re-layouts: 36.2 us -> 7.63 us
  between operations: 20.3 us -> 1.47 us
    another operation x36 -> x0, other arithmetic: 225 us -> none  [the longest x25 140 us: factor_solve(): factor = lax.linalg.cholesky(matrix)]
    ppermute x44 -> x0, waiting for transfers between devices: 171 us -> none  [the longest x22 110 us: extended(): lax.ppermute(head, axis, [((i + 1) % count, i) for i in range(ends)])]
    pallas_call x0 -> x7, Pallas kernels: none -> 98.9 us  [the longest x1 32.5 us: scatter(): pl.pallas_call(functools.partial(scatter_kernel, plan), out_shape=jax.Sha...]
    ppermute x44 -> x0, starting transfers between devices: 77.6 us -> none  [the longest x22 49 us: extended(): lax.ppermute(tail, axis, [(i, (i + 1) % count) for i in range(ends)])]
    psum x1 -> x0, waiting for transfers between devices: 34.9 us -> none  [body(): lax.psum((jnp.einsum('in,im->nm', own_link, link_solved, precision=HIGH)...]
    all_gather x2 -> x0, blocking collectives: 30.9 us -> none  [the longest x1 22.9 us: body(): lax.all_gather(link_strip, ('space', 'tm'), axis=0, tiled=True)]
    another operation x44 -> x0, matrix products: 24.6 us -> none  [the longest x8 9.52 us: factor_solve(): factor = lax.linalg.cholesky(matrix)]
    dot_general x29 -> x0, matrix products: 22.8 us -> none  [the longest x6 4.54 us: block_apply(): return jnp.einsum('tsij,tsjc->tsic', inverse, field, precision=HIGH)]
  transfers between devices with their start and end apart: 47 -> 0, of which waited for: 26 -> 0; matrix products, arithmetic and copies ran while one was open for 4% -> 0% of each run, Pallas kernels for 0% -> 0%
where the time goes in v1:
time: 113 us; the launch traced here: 112 us
  Pallas kernels  98.9 us (88%)
  local copies, waits for them, and re-layouts  7.63 us (7%)
  other arithmetic  4.5 us (4%)
  between operations  1.47 us (1%)
    pallas_call x1, Pallas kernels, scatter(): pl.pallas_call(functools.partial(scatter_kernel, plan), out_shape=jax.Sha...  32.5 us
    pallas_call x1, Pallas kernels, gather(): pl.pallas_call(functools.partial(gather_kernel, plan, count), out_shape=[...  26.1 us
    pallas_call x1, Pallas kernels, body(): local_call(functools.partial(leaf_kernel, neighbours(plan, times, cells),...  16.2 us
    pallas_call x1, Pallas kernels, body(): local_call(root_kernel, jax.ShapeDtypeStruct((plan.members, 8, per * rows...  10.1 us
    pallas_call x1, Pallas kernels, body(): local_call(parent_kernel, [jax.ShapeDtypeStruct((size, roots + LANES), F3...  7.37 us
    pallas_call x1, Pallas kernels, body(): local_call(block_kernel, jax.ShapeDtypeStruct((per, rows, rows), F32), 1)  4.63 us

profile of v1, /device:TPU:0, one launch (start us, length us, event | category | flops | bytes accessed | tf_op | source)
XLA Modules:
  0.0 112.5 jit_solution(4728913264095455531)
XLA Ops:
  0.6 0.0 copy-start
  1.4 0.8 copy-done
  2.2 0.7 dynamic-slice_bitcast_fusion.refs_2_
  3.0 1.6 %dynamic-slice_bitcast_fusion.1.refs_3_ = f32[128,256]{1,0:T(8,128)} fusion(f32[8,128,256]{2,1,0:T(8,128)} %param.19, s32[]{:T(128)S(6)} %select_n.11), kind=kLoop, calls=%fused_computation.2 | loop fusion | bytes 262148 | tf_op jit(solution)/shard_map/jit(dynamic_index_in_dim)/squeeze | solution.py:471
  4.5 0.7 constant_dynamic-slice_fusion.1
  5.2 0.7 add_bitcast_fusion
  5.9 0.7 multiply_multiply_fusion
  6.6 1.3 %select_maximum_fusion.refs_4_ = f32[8,128]{1,0:T(8,128)} fusion(f32[1,128]{1,0:T(1,128)S(1)} %constant_dynamic-slice_fusion.1, f32[2,128]{1,0:T(2,128)S(1)} %multiply_multiply_fusion, f32[2,128]{1,0:T(2,128)} %bitcast.33), kind=kLoop, calls=%fused_computation.3 | loop fusion | flops 6144 | bytes 6656 | tf_op jit(solution)/shard_map/concatenate | solution.py:472
  7.9 1.8 %bitcast_convert_fusion.refs_0_ = f32[2,128,512]{2,1,0:T(8,128)} fusion(bf16[1,2,1,128,512]{4,3,2,1,0:T(8,128)(2,1)} %param.11), kind=kLoop, calls=%fused_computation | loop fusion | flops 131072 | bytes 786432 | tf_op jit(solution)/shard_map/convert_element_type | solution.py:463
  9.7 4.6 %shard_map.130.refs_1_ = f32[2,128,128]{2,1,0:T(8,128)} custom-call(f32[2,128,128]{2,1,0:T(8,128)} %bitcast.30), custom_call_target="tpu_custom_call" | custom-call | tf_op jit(solution)/shard_map/pallas_call | solution.py:465
  14.3 26.1 %shard_map.131 = (f32[4,2,128,512]{3,2,1,0:T(8,128)}, f32[4,2,128,128]{3,2,1,0:T(8,128)}, f32[4,128,512]{2,1,0:T(8,128)}, f32[4,128,256]{2,1,0:T(8,128)}, f32[4,8,128]{2,1,0:T(8,128)}) custom-call(f32[2,128,512]{2,1,0:T(8,128)} %bitcast_convert_fusion.refs_0_, f32[2,128,128]{2,1,0:T(8,128)} %shard_map.130.refs_1_, ...), custom_call_target="tpu_custom_call" | custom-call | tf_op jit(solution)/shard_map/pallas_call | solution.py:272
  40.4 16.2 %shard_map.132 = (f32[512,640]{1,0:T(8,128)}, f32[8,128,640]{2,1,0:T(8,128)}) custom-call(f32[4,2,128,512]{3,2,1,0:T(8,128)} %get-tuple-element.14.coupling_ref, f32[4,2,128,128]{3,2,1,0:T(8,128)} %get-tuple-element.15.inverse_ref, f32[4,8,128]{2,1,0:T(8,128)} %get-tuple-element.16.vector_ref), custom_call_target="tpu_custom_call" | custom-call | tf_op jit(solution)/shard_map/pallas_call | solution.py:485
  56.6 1.3 %slice_bitcast_fusion.right_ref = f32[1,512]{1,0:T(1,128)} fusion(f32[4,8,128]{2,1,0:T(8,128)} %get-tuple-element.16.vector_ref), kind=kLoop, calls=%fused_computation.6 | loop fusion | bytes 4096 | tf_op jit(solution)/shard_map/reshape;squeeze | solution.py:499
  57.9 7.4 %shard_map.133 = (f32[512,384]{1,0:T(8,128)}, f32[264,256]{1,0:T(8,128)}) custom-call(f32[512,640]{1,0:T(8,128)} %get-tuple-element.17.schur_ref, f32[512,512]{1,0:T(8,128)} %bitcast.28, f32[1,512]{1,0:T(1,128)} %slice_bitcast_fusion.right_ref, f32[512,256]{1,0:T(8,128)} %bitcast.29), custom_call_target="tpu_custom_call" | custom-call | tf_op jit(solution)/shard_map/pallas_call | solution.py:500
  65.3 2.1 %shard_map.134 = (f32[256,256]{1,0:T(8,128)}, f32[8,256]{1,0:T(8,128)}) custom-call(f32[264,256]{1,0:T(8,128)} %get-tuple-element.20.term_ref), custom_call_target="tpu_custom_call" | custom-call | tf_op jit(solution)/shard_map/pallas_call | solution.py:343
  67.3 10.1 %shard_map.135.pack_ref = f32[4,8,1024]{2,1,0:T(8,128)} custom-call(f32[256,256]{1,0:T(8,128)} %matrix_ref.1, f32[256,256]{1,0:T(8,128)} %get-tuple-element.21.term_ref, f32[8,256]{1,0:T(8,128)} %get-tuple-element.22.vector_ref, f32[1,256]{1,0:T(1,128)} %bitcast.31, f32[512,384]{1,0:T(8,128)} %get-tuple-element.23.solution_ref, ...), custom_call_target="tpu_custom_call" | custom-call | tf_op jit(solution)/shard_map/pallas_call | solution.py:511
  77.4 32.5 %shard_map.136 = f32[8,1024]{1,0:T(8,128)} custom-call(f32[4,8,1024]{2,1,0:T(8,128)} %shard_map.135.pack_ref), custom_call_target="tpu_custom_call" | custom-call | tf_op jit(solution)/shard_map/pallas_call | solution.py:394
  109.9 0.8 slice.20
  110.7 0.5 constant_dynamic-slice_fusion
  111.2 1.3 %fusion = (f32[1,256]{1,0:T(1,128)}, f32[1,2,1,128]{3,2,1,0:T(1,128)}) fusion(f32[8,1024]{1,0:T(8,128)} %shard_map.136), kind=kLoop, calls=%fused_computation.12 | loop fusion | bytes 4096 | tf_op jit(solution)/shard_map/slice | solution.py:520
Async XLA Ops:
  0.6 1.6 %copy-start = (f32[8,128,512]{2,1,0:T(8,128)S(1)}, f32[8,128,512]{2,1,0:T(8,128)}, u32[]{:S(2)}) copy-start(f32[8,128,512]{2,1,0:T(8,128)} %param.17) | copy-start | bytes 6291460

commit v2 on v1

v2 whole, which is shorter than its diff:
```python
import functools

import jax
import jax.numpy as jnp
from jax import lax
from jax.experimental import pallas as pl
from jax.experimental.pallas import tpu as pltpu
from jax.sharding import PartitionSpec as P

PARENTS = 8
ITERS = 6
LANES = 128
F32 = jnp.float32
BF16 = jnp.bfloat16
HIGH = lax.Precision.HIGHEST
MESH = pl.DeviceIdType.MESH
VMEM = pl.BlockSpec(memory_space=pltpu.VMEM)
ANY = pl.BlockSpec(memory_space=pl.ANY)
LIMIT = 56 * 1024 * 1024
SETTLED = 3e-4
NN = ((1,), (0,))
NT = ((1,), (1,))
TN = ((0,), (0,))


def full_dot(a, b, dims=NN):
    return lax.dot_general(a, b, (dims, ((), ())), precision=HIGH, preferred_element_type=F32)


def fast_dot(a, b, dims=NN):
    return lax.dot_general(a, b, (dims, ((), ())), preferred_element_type=F32)


def halves(x):
    top = x.astype(BF16)
    return top, (x - top.astype(F32)).astype(BF16)


def as_columns(row):
    return jnp.broadcast_to(row, (LANES, LANES)).T


def near_dot(a, b, dims=NN):
    a_top, a_low = halves(a)
    b_top, b_low = halves(b)
    return fast_dot(a_top, b_top, dims) + fast_dot(a_top, b_low, dims) + fast_dot(a_low, b_top, dims)


def spd_inverse(matrix, steps=None):
    size = matrix.shape[0]
    row = lax.broadcasted_iota(jnp.int32, (size, size), 0)
    column = lax.broadcasted_iota(jnp.int32, (size, size), 1)
    identity = jnp.where(row == column, 1.0, 0.0).astype(F32)
    square = near_dot(matrix, matrix)
    plain = jnp.max(jnp.sum(jnp.abs(matrix), axis=0, keepdims=True), axis=1, keepdims=True)
    squared = jnp.max(jnp.sum(jnp.abs(square), axis=0, keepdims=True), axis=1, keepdims=True)
    bound = jnp.maximum(jnp.minimum(plain, jnp.sqrt(squared)) * 1.0001, 1.0)
    total, spread = bound + 1.0, bound - 1.0
    scale = 1.0 / (2.0 * total * total - spread * spread)
    alpha, beta = 8.0 * total * scale, 8.0 * scale
    start = alpha * identity - beta * matrix
    residual = identity - alpha * matrix + beta * square

    def grow(x, r):
        both = near_dot(jnp.concatenate([x, r], axis=0), r)
        return x + both[:size], both[size:]

    def correct(_, x):
        return x + near_dot(x, identity - full_dot(matrix, x))

    if steps is not None:
        x, _ = lax.fori_loop(0, steps, lambda _, state: grow(*state), (start, residual))
        return lax.fori_loop(0, 2, correct, x)
    rho = jnp.max(spread * spread * scale)
    largest = jnp.max(bound)
    _, _, x, _ = lax.while_loop(
        lambda state: (state[0] > SETTLED) & (state[1] < 32),
        lambda state: (state[0] * state[0], state[1] + 1) + grow(*state[2:]),
        (rho, jnp.int32(0), start, residual),
    )
    rounds = 1 + (largest > 50.0).astype(jnp.int32) + (largest > 1000.0).astype(jnp.int32)
    return lax.fori_loop(0, rounds, correct, x)


def steps_for(bound):
    rho = (bound - 1.0) ** 2 / (2.0 * (bound + 1.0) ** 2 - (bound - 1.0) ** 2)
    steps = 0
    while rho > SETTLED:
        rho, steps = rho * rho, steps + 1
    return steps


def parent_kernel(plan, schur_ref, diagonal_ref, beside_ref, right_ref, link_ref, solution_ref, term_ref):
    half = diagonal_ref.shape[1]
    size = 2 * half
    roots = link_ref.shape[1]
    scen, _ = plan.here()
    near = lax.div(plan.leader(scen), plan.members // 2)
    right = jnp.concatenate(
        [as_columns(right_ref[:, pl.ds(c, LANES)]) for c in range(0, size, LANES)], axis=0
    )
    sides = jnp.concatenate([link_ref[...], schur_ref[:, pl.ds(half, LANES)] - right], axis=1)
    a, b = pl.ds(0, half), pl.ds(half, half)
    behind = pl.ds(half + LANES, half)
    beside = beside_ref[...]
    h11 = diagonal_ref[a, :] + schur_ref[a, a]
    h12 = jnp.where(near == 0, beside, beside.T) + schur_ref[a, behind]
    h22 = diagonal_ref[b, :] + schur_ref[b, behind]
    x11 = spd_inverse(h11)
    eliminated = full_dot(x11, jnp.concatenate([h12, sides[:half]], axis=1))
    rest = full_dot(h12, eliminated, TN)
    x22 = spd_inverse(h22 - rest[:, :half])
    lower = near_dot(x22, sides[half:] - rest[:, half:])
    upper = eliminated[:, half:] - near_dot(eliminated[:, :half], lower)
    solution_ref[a, :] = upper
    solution_ref[b, :] = lower
    term_ref[...] = near_dot(solution_ref[...], link_ref[...], TN)[:roots + 8]


def root_kernel(matrix_ref, term_ref, vector_ref, right_ref, solution_ref, solved_ref, pack_ref):
    roots = matrix_ref.shape[0]
    size = solution_ref.shape[0]
    groups = pack_ref.shape[0]
    count, rows, wide = solved_ref.shape
    per = count // groups
    share = size // groups
    inverse = spd_inverse(matrix_ref[...] + term_ref[...])
    root = full_dot(right_ref[...] - vector_ref[...], inverse)
    lane = lax.broadcasted_iota(jnp.int32, (8, LANES), 1)
    unit = jnp.where(lane == 0, 1.0, 0.0).astype(F32)
    parent = full_dot(jnp.concatenate([root, unit], axis=1), solution_ref[...], NT)
    mix = jnp.concatenate([-parent[:, :size // 2], unit, -parent[:, size // 2:]], axis=1)
    for g in range(groups):
        own = solved_ref[pl.ds(g * per, per)].reshape(per * rows, wide)
        pack_ref[g, :, pl.ds(0, per * rows)] = near_dot(mix, own, NT)
        pack_ref[g, :, pl.ds(per * rows, roots)] = root
        pack_ref[g, :, pl.ds(per * rows + roots, share)] = parent[:, g * share:(g + 1) * share]


class Plan:
    def __init__(self, mesh):
        self.scen, self.space, self.tm = (mesh.shape[name] for name in ("scen", "space", "tm"))
        self.members = self.space * self.tm
        self.siblings = self.scen // PARENTS

    def leader(self, scen):
        middle = self.members // 2
        if self.siblings == 1:
            return middle - lax.rem(scen, 2)
        return middle + 0 * scen

    def device(self, scen, member):
        return (scen, lax.div(member, self.tm), lax.rem(member, self.tm))

    def here(self):
        return lax.axis_index("scen"), lax.axis_index("space") * self.tm + lax.axis_index("tm")


def leaf_kernel(plan, beside, per, coupling_ref, rhs_ref, conductance_ref, compressor_ref, blocks_ref,
                parent_of_ref, parent_mat_ref, parent_rhs_ref, link_ref,
                schur_ref, solved_ref, right_ref, all_diagonal, all_beside, all_link,
                own_lines, own_half, own_inverse, own_diagonal, own_beside, own_link,
                all_lines, all_half, all_inverse,
                field, plain, scaled, weight_ref, bits, send, receive, local):
    count = len(beside)
    members = plan.members
    times, cells = coupling_ref.shape[1:3]
    half = coupling_ref.shape[-1] // 2
    share = parent_rhs_ref.shape[1]
    scen, member = plan.here()
    lead = plan.leader(scen)
    leads = member == lead
    close = lax.div(member, members // 2) == lax.div(lead, members // 2)
    place = lax.rem(member, members // 2)
    barrier = pltpu.get_barrier_semaphore()
    LINES, FIRST, INVERSE, SECOND, DIAGONAL, LINK, BESIDE = range(7)

    def remote(kind, at, slot):
        source, target = {
            LINES: (own_lines, all_lines.at[at]),
            FIRST: (own_half.at[0], all_half.at[0, at]),
            INVERSE: (own_inverse, all_inverse.at[at]),
            SECOND: (own_half.at[1], all_half.at[1, at]),
            DIAGONAL: (own_diagonal, all_diagonal.at[at]),
            LINK: (own_link, all_link.at[at]),
            BESIDE: (own_beside, all_beside.at[lax.rem(at, members // 2)]),
        }[kind]
        return pltpu.make_async_remote_copy(
            src_ref=source, dst_ref=target, send_sem=send.at[kind], recv_sem=receive.at[kind, slot],
            device_id=plan.device(scen, lead), device_id_type=MESH,
        )

    others = [lax.rem(lead + k, members) for k in range(1, members)]
    slot = lax.rem(member - lead + members, members) - 1

    @pl.when(leads)
    def _():
        for other in others:
            pl.semaphore_signal(
                barrier, inc=1, device_id=plan.device(scen, other), device_id_type=MESH
            )

    @pl.when(jnp.logical_not(leads))
    def _():
        pl.semaphore_signal(barrier, inc=1, device_id=plan.device(scen, lead), device_id_type=MESH)

    label = parent_of_ref[0]
    own_lines[...] = jnp.zeros_like(own_lines)
    for k in range(per):
        t, c = divmod(k, cells)
        own_lines[k:k + 1, :] = rhs_ref[0, t, c:c + 1, :]
        doubled = 1.0 + compressor_ref[0, t, c].astype(F32)
        own_lines[per + k:per + k + 1, :] = conductance_ref[0, t, c:c + 1, :] * doubled * 0.5
        for j in range(2):
            own_half[j, k] = coupling_ref[0, t, c, :, pl.ds(j * half, half)].astype(F32)
    own_lines[2 * per:2 * per + 1, pl.ds(0, share)] = parent_rhs_ref[pl.ds(label, 1), :]

    @pl.when(jnp.logical_not(leads))
    def _():
        pl.semaphore_wait(barrier, 1)
        remote(LINES, member, slot).start()
        remote(FIRST, member, slot).start()

    rows = blocks_ref.shape[-1]
    zero = jnp.zeros((rows, rows), F32)
    for i in range(0, per, 2):
        j = min(i + 1, per - 1)
        first = blocks_ref[0, i // cells, i % cells]
        second = blocks_ref[0, j // cells, j % cells]
        pair = jnp.concatenate(
            [jnp.concatenate([first, zero], axis=1), jnp.concatenate([zero, second], axis=1)], axis=0
        )
        found = spd_inverse(pair, steps_for(8.0 * rows))
        own_inverse[i] = found[:rows, :rows]
        own_inverse[j] = found[rows:, rows:]
    strip = parent_mat_ref[label]
    lower = lax.div(member, members // 2) == 0
    own_diagonal[...] = jnp.where(lower, strip[:, :half], strip[:, half:])
    own_beside[...] = jnp.where(lower, strip[:, half:], strip[:, :half])
    own_link[...] = link_ref[label]

    @pl.when(jnp.logical_not(leads))
    def _():
        remote(INVERSE, member, slot).start()
        remote(SECOND, member, slot).start()
        for kind in (LINES, FIRST, INVERSE, SECOND):
            remote(kind, member, slot).wait_send()
        remote(DIAGONAL, member, slot).start()
        remote(LINK, member, slot).start()

        @pl.when(close)
        def _():
            remote(BESIDE, member, slot).start()
            remote(BESIDE, member, slot).wait_send()

        remote(DIAGONAL, member, slot).wait_send()
        remote(LINK, member, slot).wait_send()

    def arrived(*kinds):
        for kind in kinds:
            for k, other in enumerate(others):
                remote(kind, other, k).wait_recv()

    def stacked(matrix):
        top, low = halves(matrix)
        return jnp.concatenate([top, low, top], axis=1)

    def stack(x):
        top, low = halves(x)
        return jnp.concatenate([top, top, low], axis=0)

    def source(n, units):
        g, k = divmod(n, per)
        parts = []
        for unit in units:
            if unit is None:
                parts.append(as_columns(all_lines[g, k:k + 1, :]))
            else:
                j, start = divmod(unit, half)
                parts.append(all_half[j, g, k, :, pl.ds(start, LANES)])
        return jnp.concatenate(parts, axis=1)

    def around(at, n):
        total = field[at, beside[n][0]]
        for m in beside[n][1:]:
            total = total + field[at, m]
        return total

    last = (ITERS - 2) % 2

    def solve(units, start):
        width = LANES * len(units)
        here = pl.ds(start, width)

        def spread(n):
            return jnp.concatenate([weight_ref[n]] * len(units), axis=1)

        for n in range(count):
            first = spread(n) * fast_dot(plain[n], stack(source(n, units)))
            field[0, n, :, pl.ds(0, width)] = first
            solved_ref[n, :, here] = first

        def sweep(k, carry):
            now = lax.rem(k, 2)
            for n in range(count):
                moved = fast_dot(scaled[n], stack(around(now, n)[:, :width]))
                field[1 - now, n, :, pl.ds(0, width)] = solved_ref[n, :, here] + moved
            return carry

        lax.fori_loop(0, ITERS - 2, sweep, 0)
        for n in range(count):
            drive = source(n, units) + spread(n) * around(last, n)[:, :width]
            solved_ref[n, :, here] = fast_dot(plain[n], stack(drive))

    def solve_all(units, start):
        step = field.shape[-1] // LANES
        for i in range(0, len(units), step):
            solve(units[i:i + step], start + i * LANES)

    def product(j, start, width):
        out = None
        chunk = min(count, 8)
        for c in range(0, count, chunk):
            part = solved_ref[pl.ds(c, chunk), :, pl.ds(start, width)]
            top, low = halves(part.reshape(chunk * LANES, width))
            own = bits[j, pl.ds(c * LANES, chunk * LANES), :]
            part = fast_dot(own, top, TN) + fast_dot(own, low, TN)
            out = part if out is None else out + part
        return out

    def cast(j):
        for n in range(count):
            g, k = divmod(n, per)
            bits[j, pl.ds(n * LANES, LANES), :] = all_half[j, g, k].astype(BF16)

    @pl.when(leads)
    def _():
        own = [
            pltpu.make_async_copy(own_diagonal, all_diagonal.at[member], local.at[0]),
            pltpu.make_async_copy(own_link, all_link.at[member], local.at[1]),
            pltpu.make_async_copy(own_beside, all_beside.at[place], local.at[2]),
        ]
        for copy in own:
            copy.start()
        all_lines[member] = own_lines[...]
        all_inverse[member] = own_inverse[...]
        for j in range(2):
            all_half[j, member] = own_half[j]
        pl.semaphore_wait(barrier, members - 1)
        arrived(LINES, INVERSE)
        for n in range(count):
            g, k = divmod(n, per)
            weight_row = all_lines[g, per + k:per + k + 1, :]
            weight = as_columns(weight_row)
            inverse = all_inverse[g, k]
            weight_ref[n] = weight
            plain[n] = stacked(inverse)
            scaled[n] = stacked(weight * inverse * weight_row)
        for g in range(members):
            right_ref[:, pl.ds(g * share, share)] = all_lines[g, 2 * per:2 * per + 1, pl.ds(0, share)]
        arrived(FIRST)
        cast(0)
        solve_all(list(range(0, half, LANES)) + [None], 0)
        schur_ref[pl.ds(0, half), pl.ds(0, half + LANES)] = product(0, 0, half + LANES)
        arrived(SECOND)
        cast(1)
        solve_all(list(range(half, 2 * half, LANES)), half + LANES)
        schur_ref[pl.ds(0, half), pl.ds(half + LANES, half)] = product(0, half + LANES, half)
        schur_ref[pl.ds(half, half), pl.ds(half, half + LANES)] = product(1, half, half + LANES)
        arrived(DIAGONAL, LINK)
        for k, other in enumerate(others):
            @pl.when(lax.div(other, members // 2) == lax.div(lead, members // 2))
            def _():
                remote(BESIDE, other, k).wait_recv()
        for copy in own:
            copy.wait()


def solve_leaves(plan, arrays):
    coupling, _, _, _, _, _, parent_mat, _, link = arrays
    _, times, cells, rows, size = coupling.shape
    share, roots = link.shape[1:]
    per, members, half = times * cells, plan.members, size // 2
    count, wide = members * per, size + LANES
    SMEM = pl.BlockSpec(memory_space=pltpu.SMEM)
    lines = -(-(2 * per + 1) // 8) * 8
    shape = lambda *sizes: jax.ShapeDtypeStruct(sizes, F32)
    return pl.pallas_call(
        functools.partial(leaf_kernel, plan, neighbours(plan, times, cells), per),
        out_shape=[
            shape(size, wide),
            shape(count, rows, wide),
            shape(1, size),
            shape(members, share, half),
            shape(members // 2, share, half),
            shape(members, share, roots),
        ],
        in_specs=[VMEM, VMEM, VMEM, SMEM, VMEM, SMEM, VMEM, VMEM, VMEM],
        out_specs=[VMEM, VMEM, VMEM, ANY, ANY, ANY],
        scratch_shapes=[
            pltpu.VMEM((lines, LANES), F32),
            pltpu.VMEM((2, per, rows, half), F32),
            pltpu.VMEM((per, rows, rows), F32),
            pltpu.VMEM((share, half), F32),
            pltpu.VMEM((share, half), F32),
            pltpu.VMEM((share, roots), F32),
            pltpu.VMEM((members, lines, LANES), F32),
            pltpu.VMEM((2, members, per, rows, half), F32),
            pltpu.VMEM((members, per, rows, rows), F32),
            pltpu.VMEM((2, count, rows, half + LANES if count <= 8 else LANES), F32),
            pltpu.VMEM((count, rows, 3 * rows), BF16),
            pltpu.VMEM((count, rows, 3 * rows), BF16),
            pltpu.VMEM((count, rows, LANES), F32),
            pltpu.VMEM((2, count * rows, half), BF16),
            pltpu.SemaphoreType.DMA((7,)),
            pltpu.SemaphoreType.DMA((7, members - 1)),
            pltpu.SemaphoreType.DMA((3,)),
        ],
        compiler_params=pltpu.CompilerParams(
            collective_id=0, has_side_effects=True, vmem_limit_bytes=LIMIT
        ),
    )(*arrays)


def sum_kernel(plan, term_ref, total_ref, vector_ref, strips, vectors, whole,
               send, receive):
    scen, member = plan.here()
    lead = plan.leader(scen)
    count = plan.scen
    roots = whole.shape[0]
    rows = roots // count
    barrier = pltpu.get_barrier_semaphore()

    @pl.when(member == lead)
    def _():
        peers = [lax.rem(scen + k, count) for k in range(1, count)]
        devices = [plan.device(peer, plan.leader(peer)) for peer in peers]
        for device in devices:
            pl.semaphore_signal(barrier, inc=1, device_id=device, device_id_type=MESH)
        mine = pl.ds(pl.multiple_of(scen * rows, rows), rows)
        strips[scen] = term_ref[mine, :]
        vectors[scen] = term_ref[pl.ds(roots, 8), :]
        pl.semaphore_wait(barrier, count - 1)

        def remote(kind, k, source, target):
            return pltpu.make_async_remote_copy(
                src_ref=source, dst_ref=target, send_sem=send.at[kind, k],
                recv_sem=receive.at[kind, k], device_id=devices[k], device_id_type=MESH,
            )

        copies = []
        for k, peer in enumerate(peers):
            theirs = pl.ds(pl.multiple_of(peer * rows, rows), rows)
            copies.append(remote(0, k, term_ref.at[theirs, :], strips.at[scen]))
            copies.append(remote(1, k, term_ref.at[pl.ds(roots, 8), :], vectors.at[scen]))
        for copy in copies:
            copy.start()
        for copy in copies:
            copy.wait()
        total = strips[0]
        vector = vectors[0]
        for s in range(1, count):
            total = total + strips[s]
            vector = vector + vectors[s]
        vector_ref[...] = vector
        whole[mine, :] = total
        copies = [remote(2, k, whole.at[mine, :], whole.at[mine, :]) for k in range(count - 1)]
        for copy in copies:
            copy.start()
        for copy in copies:
            copy.wait()
        total_ref[...] = whole[...]

    @pl.when(member != lead)
    def _():
        total_ref[...] = jnp.zeros_like(total_ref)
        vector_ref[...] = jnp.zeros_like(vector_ref)


def sum_terms(plan, term):
    roots = term.shape[1]
    return pl.pallas_call(
        functools.partial(sum_kernel, plan),
        out_shape=[jax.ShapeDtypeStruct((roots, roots), F32), jax.ShapeDtypeStruct((8, roots), F32)],
        in_specs=[VMEM],
        out_specs=[VMEM] * 2,
        scratch_shapes=[
            pltpu.VMEM((plan.scen, roots // plan.scen, roots), F32),
            pltpu.VMEM((plan.scen, 8, roots), F32),
            pltpu.VMEM((roots, roots), F32),
            pltpu.SemaphoreType.DMA((3, plan.scen - 1)),
            pltpu.SemaphoreType.DMA((3, plan.scen - 1)),
        ],
        compiler_params=pltpu.CompilerParams(collective_id=1, has_side_effects=True),
    )(term)


def scatter_kernel(plan, pack_ref, leaf_ref, parent_ref, root_ref, landed, send, receive):
    times, cells = leaf_ref.shape[1:3]
    roots, share = root_ref.shape[0], parent_ref.shape[1]
    base = times * cells * LANES

    def write(line):
        for k in range(times * cells):
            t, c = divmod(k, cells)
            leaf_ref[0, t, c:c + 1, :] = line[:, k * LANES:(k + 1) * LANES]
        root_ref[...] = line[0, base:base + roots]
        parent_ref[...] = line[:, base + roots:base + roots + share]

    scen, member = plan.here()
    lead = plan.leader(scen)
    barrier = pltpu.get_barrier_semaphore()

    def remote(k, other):
        return pltpu.make_async_remote_copy(
            src_ref=pack_ref.at[other], dst_ref=landed, send_sem=send.at[k],
            recv_sem=receive, device_id=plan.device(scen, other), device_id_type=MESH,
        )

    @pl.when(member != lead)
    def _():
        pl.semaphore_signal(barrier, inc=1, device_id=plan.device(scen, lead), device_id_type=MESH)
        pl.semaphore_wait(barrier, 1)
        remote(0, lead).wait_recv()
        write(landed[0:1, :])

    @pl.when(member == lead)
    def _():
        others = [lax.rem(lead + k, plan.members) for k in range(1, plan.members)]
        for other in others:
            pl.semaphore_signal(
                barrier, inc=1, device_id=plan.device(scen, other), device_id_type=MESH
            )
        pl.semaphore_wait(barrier, plan.members - 1)
        copies = [remote(k, other) for k, other in enumerate(others)]
        for copy in copies:
            copy.start()
        write(pack_ref[member][0:1, :])
        for copy in copies:
            copy.wait_send()


def scatter(plan, pack, shapes):
    return pl.pallas_call(
        functools.partial(scatter_kernel, plan),
        out_shape=[jax.ShapeDtypeStruct(shape, F32) for shape in shapes],
        in_specs=[VMEM],
        out_specs=[VMEM] * 3,
        scratch_shapes=[
            pltpu.VMEM(pack.shape[1:], F32),
            pltpu.SemaphoreType.DMA((plan.members - 1,)),
            pltpu.SemaphoreType.DMA,
        ],
        compiler_params=pltpu.CompilerParams(collective_id=2, has_side_effects=True),
    )(pack)


def local_call(kernel, out_shape, count, scratch=()):
    many = isinstance(out_shape, list)
    return pl.pallas_call(
        kernel,
        out_shape=out_shape,
        in_specs=[VMEM] * count,
        out_specs=[VMEM] * len(out_shape) if many else VMEM,
        scratch_shapes=list(scratch),
        compiler_params=pltpu.CompilerParams(vmem_limit_bytes=LIMIT),
    )


def from_partner(block, axis, bit):
    count = lax.axis_size(axis)
    route = []
    for low in range(count):
        high = low | 1 << bit
        if high != low and high < count:
            route += [(low, high), (high, low)]
    return lax.ppermute(block, axis, route)


def neighbours(plan, times, cells):
    place = {}
    for g in range(plan.members):
        for t in range(times):
            for s in range(cells):
                at = ((g % plan.tm) * times + t, (g // plan.tm) * cells + s)
                place[at] = (g * times + t) * cells + s
    found = [None] * len(place)
    for (t, s), n in place.items():
        sides = [(t + 1, s), (t - 1, s), (t, s + 1), (t, s - 1)]
        found[n] = [place[side] for side in sides if side in place]
    return found


def body(
    plan,
    coupling,
    leaf_rhs,
    conductance,
    compressor,
    blocks,
    parent_of,
    parent_mat,
    parent_rhs,
    link,
    root_mat,
    root_rhs,
):
    _, times, cells, rows, size = coupling.shape
    per = times * cells
    roots = root_rhs.shape[0]
    share = parent_rhs.shape[1]
    schur, solved, right, diagonal, beside, all_link = solve_leaves(
        plan,
        [coupling, leaf_rhs, conductance, compressor, blocks, parent_of, parent_mat, parent_rhs, link],
    )
    for bit_index in range(plan.siblings.bit_length() - 1):
        schur = schur + from_partner(schur, "scen", bit_index)
    solution_p, term = local_call(
        functools.partial(parent_kernel, plan),
        [
            jax.ShapeDtypeStruct((size, roots + LANES), F32),
            jax.ShapeDtypeStruct((roots + 8, roots), F32),
        ],
        5,
    )(
        schur,
        diagonal.reshape(size, size // 2),
        beside.reshape(size // 2, size // 2),
        right,
        all_link.reshape(size, roots),
    )
    if plan.siblings > 1:
        term = jnp.where(lax.axis_index("scen") % plan.siblings == 0, term, 0.0)
    total, vector = sum_terms(plan, term)
    width = per * rows + roots + -(-share // LANES) * LANES
    pack = local_call(
        root_kernel, jax.ShapeDtypeStruct((plan.members, 8, width), F32), 6
    )(root_mat, total, vector, root_rhs[None], solution_p, solved)
    return scatter(plan, pack, [leaf_rhs.shape, (1, share), (roots,)])


def solution(mesh):
    return jax.shard_map(
        functools.partial(body, Plan(mesh)),
        mesh=mesh,
        in_specs=(
            P("scen", "tm", "space", None, None),
            P("scen", "tm", "space", None),
            P("scen", "tm", "space", None),
            P("scen", "tm", "space"),
            P("scen", "tm", "space", None, None),
            P("scen"),
            P(None, ("space", "tm"), None),
            P(None, ("space", "tm")),
            P(None, ("space", "tm"), None),
            P(),
            P(),
        ),
        out_specs=(P("scen", "tm", "space", None), P("scen", ("space", "tm")), P()),
        check_vma=False,
    )
```

time: 113 us -> 83.4 us (0.74)
  Pallas kernels: 98.9 us -> 77 us
  other arithmetic: 4.5 us -> 0 us
  local copies, waits for them, and re-layouts: 7.63 us -> 4.8 us
    pallas_call x6 -> x4, Pallas kernels: 96.8 us -> 75 us  [the longest x1 30 us: scatter(): pl.pallas_call(functools.partial(scatter_kernel, plan), out_shape=[jax.Sh...]
    unnamed x2 -> x4, local copies, waits for them, and re-layouts: 0.81 us -> 4.8 us
    squeeze x2 -> x0, local copies, waits for them, and re-layouts: 2.28 us -> none  [the longest x1 1.56 us: body(): own_link = lax.dynamic_index_in_dim(link, label, 0, keepdims=False)]
    slice x2 -> x0, local copies, waits for them, and re-layouts: 2.04 us -> none  [the longest x1 1.28 us: body(): return (leaf_move, parent_at_leaf, line[per * rows + size:])]
    convert_element_type x1 -> x0, other arithmetic: 1.81 us -> none  [body(): dense = coupling.reshape(per, rows, size).astype(F32)]
    another operation x1 -> x0, local copies, waits for them, and re-layouts: 1.31 us -> none  [body(): right = all_lines[:, 2 * per, :share].reshape(1, size)]
    concatenate x1 -> x0, other arithmetic: 1.28 us -> none  [body(): jnp.concatenate([leaf_rhs.reshape(per, rows), weight.reshape(per, rows),...]
    dynamic_slice x2 -> x0, local copies, waits for them, and re-layouts: 1.2 us -> none  [the longest x1 0.69 us: body(): own_rhs = lax.dynamic_index_in_dim(parent_rhs, label, 0, keepdims=True)]
where the time goes in v2:
time: 83.4 us; the launch traced here: 83.1 us
  Pallas kernels  77 us (92%)
  local copies, waits for them, and re-layouts  4.8 us (6%)
  between operations  1.3 us (2%)
    pallas_call x1, Pallas kernels, scatter(): pl.pallas_call(functools.partial(scatter_kernel, plan), out_shape=[jax.Sh...  30 us
    pallas_call x1, Pallas kernels, solve_leaves(): pl.pallas_call(functools.partial(leaf_kernel, plan, neighbours(plan, time...  29.3 us
    pallas_call x1, Pallas kernels, body(): local_call(root_kernel, jax.ShapeDtypeStruct((plan.members, 8, width), F3...  7.85 us
    pallas_call x1, Pallas kernels, body(): local_call(functools.partial(parent_kernel, plan), [jax.ShapeDtypeStruct(...  7.77 us
    unnamed x4, local copies, waits for them, and re-layouts  4.8 us
    pallas_call x1, Pallas kernels, sum_terms(): pl.pallas_call(functools.partial(sum_kernel, plan), out_shape=[jax.ShapeD...  2.07 us

profile of v2, /device:TPU:0, one launch (start us, length us, event | category | flops | bytes accessed | tf_op | source)
XLA Modules:
  0.0 83.1 jit_solution(11543976042016139558)
XLA Ops:
  1.3 1.3 %copy.14.compressor_ref = s32[1,2,1]{2,1,0:T(2,128)} copy(s32[1,2,1]{1,2,0:T(1,128)} %param.14) | data formatting | bytes 16 | tf_op args[3]
  2.6 29.3 %shard_map.130 = (f32[512,640]{1,0:T(8,128)}, f32[8,128,640]{2,1,0:T(8,128)}, f32[1,512]{1,0:T(1,128)}, f32[4,128,256]{2,1,0:T(8,128)}, f32[2,128,256]{2,1,0:T(8,128)}, /*index=5*/f32[4,128,256]{2,1,0:T(8,128)}) custom-call(bf16[1,2,1,128,512]{4,3,2,1,0:T(8,128)(2,1)} %coupling_ref.1, f32[1,2,1,128]{3,2,1,0:T(1,128)} %rhs_ref.1, ...), custom_call_target="tpu_custom_call" | custom-call | tf_op jit(solution)/shard_map/pallas_call | solution.py:388
  31.9 7.8 %shard_map.131 = (f32[512,384]{1,0:T(8,128)}, f32[264,256]{1,0:T(8,128)}) custom-call(f32[512,640]{1,0:T(8,128)} %get-tuple-element.13.schur_ref, f32[512,256]{1,0:T(8,128)} %bitcast.4, f32[256,256]{1,0:T(8,128)} %bitcast.6, f32[1,512]{1,0:T(1,128)} %get-tuple-element.16.right_ref, f32[512,256]{1,0:T(8,128)} %bitcast.5), custom_call_target="tpu_custom_call" | custom-call | tf_op jit(solution)/shard_map/pallas_call | solution.py:618
  39.7 2.1 %shard_map.132 = (f32[256,256]{1,0:T(8,128)}, f32[8,256]{1,0:T(8,128)}) custom-call(f32[264,256]{1,0:T(8,128)} %get-tuple-element.18.term_ref), custom_call_target="tpu_custom_call" | custom-call | tf_op jit(solution)/shard_map/pallas_call | solution.py:482
  41.7 7.9 %shard_map.133.pack_ref = f32[4,8,640]{2,1,0:T(8,128)} custom-call(f32[256,256]{1,0:T(8,128)} %matrix_ref.1, f32[256,256]{1,0:T(8,128)} %get-tuple-element.19.term_ref, f32[8,256]{1,0:T(8,128)} %get-tuple-element.20.vector_ref, f32[1,256]{1,0:T(1,128)} %bitcast.7, f32[512,384]{1,0:T(8,128)} %get-tuple-element.21.solution_ref, ...), custom_call_target="tpu_custom_call" | custom-call | tf_op jit(solution)/shard_map/pallas_call | solution.py:636
  49.6 30.0 %shard_map.134 = (f32[1,2,1,128]{3,2,1,0:T(1,128)}, f32[1,128]{1,0:T(1,128)}, f32[256]{0:T(256)}) custom-call(f32[4,8,640]{2,1,0:T(8,128)} %shard_map.133.pack_ref), custom_call_target="tpu_custom_call" | custom-call | tf_op jit(solution)/shard_map/pallas_call | solution.py:544
  79.6 1.2 %copy.19 = f32[1,2,1,128]{3,2,1,0:T(1,128)} copy(f32[1,2,1,128]{3,2,1,0:T(1,128)} %get-tuple-element.26) | data formatting | bytes 2048
  80.8 1.1 %copy.20 = f32[1,128]{1,0:T(1,128)} copy(f32[1,128]{1,0:T(1,128)} %get-tuple-element.27) | data formatting | bytes 1024
  81.9 1.2 %copy.21 = f32[256]{0:T(256)} copy(f32[256]{0:T(256)} %get-tuple-element.28) | data formatting | bytes 2048

commit v3 on v2

--- a/solution.py
+++ b/solution.py
@@ -18,6 +18,7 @@
 ANY = pl.BlockSpec(memory_space=pl.ANY)
 LIMIT = 56 * 1024 * 1024
 SETTLED = 3e-4
+EXTRA = 16
 NN = ((1,), (0,))
 NT = ((1,), (1,))
 TN = ((0,), (0,))
@@ -96,22 +97,23 @@
     roots = link_ref.shape[1]
     scen, _ = plan.here()
     near = lax.div(plan.leader(scen), plan.members // 2)
+    reduced = schur_ref[pl.ds(half, 8), :][0:1] - right_ref[...]
     right = jnp.concatenate(
-        [as_columns(right_ref[:, pl.ds(c, LANES)]) for c in range(0, size, LANES)], axis=0
-    )
-    sides = jnp.concatenate([link_ref[...], schur_ref[:, pl.ds(half, LANES)] - right], axis=1)
+        [as_columns(reduced[:, c:c + LANES]) for c in range(0, size, LANES)], axis=0
+    )
     a, b = pl.ds(0, half), pl.ds(half, half)
-    behind = pl.ds(half + LANES, half)
+    behind = pl.ds(half + EXTRA, half)
+    sides = jnp.concatenate([link_ref[...], right], axis=1)
     beside = beside_ref[...]
     h11 = diagonal_ref[a, :] + schur_ref[a, a]
-    h12 = jnp.where(near == 0, beside, beside.T) + schur_ref[a, behind]
-    h22 = diagonal_ref[b, :] + schur_ref[b, behind]
+    h21 = jnp.where(near == 0, beside.T, beside) + schur_ref[behind, a]
+    h22 = diagonal_ref[b, :] + schur_ref[behind, b]
     x11 = spd_inverse(h11)
-    eliminated = full_dot(x11, jnp.concatenate([h12, sides[:half]], axis=1))
-    rest = full_dot(h12, eliminated, TN)
-    x22 = spd_inverse(h22 - rest[:, :half])
-    lower = near_dot(x22, sides[half:] - rest[:, half:])
-    upper = eliminated[:, half:] - near_dot(eliminated[:, :half], lower)
+    across = full_dot(x11, h21, NT)
+    ahead = full_dot(x11, sides[:half])
+    x22 = spd_inverse(h22 - full_dot(h21, across))
+    lower = near_dot(x22, sides[half:] - full_dot(h21, ahead))
+    upper = ahead - near_dot(across, lower)
     solution_ref[a, :] = upper
     solution_ref[b, :] = lower
     term_ref[...] = near_dot(solution_ref[...], link_ref[...], TN)[:roots + 8]
@@ -121,20 +123,34 @@
     roots = matrix_ref.shape[0]
     size = solution_ref.shape[0]
     groups = pack_ref.shape[0]
-    count, rows, wide = solved_ref.shape
-    per = count // groups
+    half = size // 2
+    width = solved_ref.shape[1] // groups
     share = size // groups
     inverse = spd_inverse(matrix_ref[...] + term_ref[...])
     root = full_dot(right_ref[...] - vector_ref[...], inverse)
     lane = lax.broadcasted_iota(jnp.int32, (8, LANES), 1)
     unit = jnp.where(lane == 0, 1.0, 0.0).astype(F32)
     parent = full_dot(jnp.concatenate([root, unit], axis=1), solution_ref[...], NT)
-    mix = jnp.concatenate([-parent[:, :size // 2], unit, -parent[:, size // 2:]], axis=1)
+    leaf = (
+        solved_ref[pl.ds(half, 8), :]
+        - near_dot(parent[:, :half], solved_ref[pl.ds(0, half), :])
+        - near_dot(parent[:, half:], solved_ref[pl.ds(half + EXTRA, half), :])
+    )
     for g in range(groups):
-        own = solved_ref[pl.ds(g * per, per)].reshape(per * rows, wide)
-        pack_ref[g, :, pl.ds(0, per * rows)] = near_dot(mix, own, NT)
-        pack_ref[g, :, pl.ds(per * rows, roots)] = root
-        pack_ref[g, :, pl.ds(per * rows + roots, share)] = parent[:, g * share:(g + 1) * share]
+        pack_ref[g, :, pl.ds(0, width)] = leaf[:, g * width:(g + 1) * width]
+        pack_ref[g, :, pl.ds(width, roots)] = root
+        pack_ref[g, :, pl.ds(width + roots, share)] = parent[:, g * share:(g + 1) * share]
+
+
+def finish_kernel(line_ref, leaf_ref, parent_ref, root_ref):
+    times, cells = leaf_ref.shape[1:3]
+    roots, share = root_ref.shape[0], parent_ref.shape[1]
+    base = times * cells * LANES
+    for k in range(times * cells):
+        t, c = divmod(k, cells)
+        leaf_ref[0, t, c:c + 1, :] = line_ref[0:1, pl.ds(k * LANES, LANES)]
+    root_ref[...] = line_ref[0, pl.ds(base, roots)]
+    parent_ref[...] = line_ref[0:1, pl.ds(base + roots, share)]
 
 
 class Plan:
@@ -161,7 +177,7 @@
                 schur_ref, solved_ref, right_ref, all_diagonal, all_beside, all_link,
                 own_lines, own_half, own_inverse, own_diagonal, own_beside, own_link,
                 all_lines, all_half, all_inverse,
-                field, plain, scaled, weight_ref, bits, send, receive, local):
+                field, plain, scaled, bits, send, receive, local):
     count = len(beside)
     members = plan.members
     times, cells = coupling_ref.shape[1:3]
@@ -212,7 +228,7 @@
         doubled = 1.0 + compressor_ref[0, t, c].astype(F32)
         own_lines[per + k:per + k + 1, :] = conductance_ref[0, t, c:c + 1, :] * doubled * 0.5
         for j in range(2):
-            own_half[j, k] = coupling_ref[0, t, c, :, pl.ds(j * half, half)].astype(F32)
+            own_half[j, k] = coupling_ref[0, t, c, :, pl.ds(j * half, half)].astype(F32).T
     own_lines[2 * per:2 * per + 1, pl.ds(0, share)] = parent_rhs_ref[pl.ds(label, 1), :]
 
     @pl.when(jnp.logical_not(leads))
@@ -261,77 +277,69 @@
             for k, other in enumerate(others):
                 remote(kind, other, k).wait_recv()
 
-    def stacked(matrix):
+    def tile(matrix):
         top, low = halves(matrix)
-        return jnp.concatenate([top, low, top], axis=1)
-
-    def stack(x):
-        top, low = halves(x)
-        return jnp.concatenate([top, top, low], axis=0)
-
-    def source(n, units):
+        return jnp.concatenate(
+            [
+                jnp.concatenate([top, low], axis=1),
+                jnp.concatenate([top, jnp.zeros_like(top)], axis=1),
+            ],
+            axis=0,
+        )
+
+    def apply(x, matrix):
+        both = fast_dot(jnp.concatenate(halves(x), axis=1), matrix)
+        return both[:, :LANES] + both[:, LANES:]
+
+    def source(j, n):
         g, k = divmod(n, per)
-        parts = []
-        for unit in units:
-            if unit is None:
-                parts.append(as_columns(all_lines[g, k:k + 1, :]))
-            else:
-                j, start = divmod(unit, half)
-                parts.append(all_half[j, g, k, :, pl.ds(start, LANES)])
-        return jnp.concatenate(parts, axis=1)
-
-    def around(at, n):
-        total = field[at, beside[n][0]]
+        if j == 1:
+            return all_half[j, g, k]
+        right = jnp.broadcast_to(all_lines[g, k:k + 1, :], (EXTRA, LANES))
+        return jnp.concatenate([all_half[j, g, k], right], axis=0)
+
+    def weight(n):
+        g, k = divmod(n, per)
+        return all_lines[g, per + k:per + k + 1, :]
+
+    def lanes(n):
+        return pl.ds(n * LANES, LANES)
+
+    def around(at, n, width):
+        total = field[at, pl.ds(0, width), lanes(beside[n][0])]
         for m in beside[n][1:]:
-            total = total + field[at, m]
+            total = total + field[at, pl.ds(0, width), lanes(m)]
         return total
 
     last = (ITERS - 2) % 2
 
-    def solve(units, start):
-        width = LANES * len(units)
-        here = pl.ds(start, width)
-
-        def spread(n):
-            return jnp.concatenate([weight_ref[n]] * len(units), axis=1)
-
+    def solve(j):
+        start, width = (half + EXTRA, half) if j else (0, half + EXTRA)
+        here, top = pl.ds(start, width), pl.ds(0, width)
         for n in range(count):
-            first = spread(n) * fast_dot(plain[n], stack(source(n, units)))
-            field[0, n, :, pl.ds(0, width)] = first
-            solved_ref[n, :, here] = first
+            g, k = divmod(n, per)
+            bits[j, :, lanes(n)] = all_half[j, g, k].astype(BF16)
+            first = weight(n) * apply(source(j, n), plain[n])
+            field[0, top, lanes(n)] = first
+            solved_ref[here, lanes(n)] = first
 
         def sweep(k, carry):
             now = lax.rem(k, 2)
             for n in range(count):
-                moved = fast_dot(scaled[n], stack(around(now, n)[:, :width]))
-                field[1 - now, n, :, pl.ds(0, width)] = solved_ref[n, :, here] + moved
+                moved = apply(around(now, n, width), scaled[n])
+                field[1 - now, top, lanes(n)] = solved_ref[here, lanes(n)] + moved
             return carry
 
         lax.fori_loop(0, ITERS - 2, sweep, 0)
         for n in range(count):
-            drive = source(n, units) + spread(n) * around(last, n)[:, :width]
-            solved_ref[n, :, here] = fast_dot(plain[n], stack(drive))
-
-    def solve_all(units, start):
-        step = field.shape[-1] // LANES
-        for i in range(0, len(units), step):
-            solve(units[i:i + step], start + i * LANES)
-
-    def product(j, start, width):
-        out = None
-        chunk = min(count, 8)
-        for c in range(0, count, chunk):
-            part = solved_ref[pl.ds(c, chunk), :, pl.ds(start, width)]
-            top, low = halves(part.reshape(chunk * LANES, width))
-            own = bits[j, pl.ds(c * LANES, chunk * LANES), :]
-            part = fast_dot(own, top, TN) + fast_dot(own, low, TN)
-            out = part if out is None else out + part
-        return out
-
-    def cast(j):
-        for n in range(count):
-            g, k = divmod(n, per)
-            bits[j, pl.ds(n * LANES, LANES), :] = all_half[j, g, k].astype(BF16)
+            drive = source(j, n) + weight(n) * around(last, n, width)
+            solved_ref[here, lanes(n)] = apply(drive, plain[n])
+
+    def product(start, width, j):
+        top, low = halves(solved_ref[pl.ds(start, width), :])
+        schur_ref[pl.ds(start, width), pl.ds(j * half, half)] = (
+            fast_dot(top, bits[j], NT) + fast_dot(low, bits[j], NT)
+        )
 
     @pl.when(leads)
     def _():
@@ -350,23 +358,18 @@
         arrived(LINES, INVERSE)
         for n in range(count):
             g, k = divmod(n, per)
-            weight_row = all_lines[g, per + k:per + k + 1, :]
-            weight = as_columns(weight_row)
             inverse = all_inverse[g, k]
-            weight_ref[n] = weight
-            plain[n] = stacked(inverse)
-            scaled[n] = stacked(weight * inverse * weight_row)
+            plain[n] = tile(inverse)
+            scaled[n] = tile(as_columns(weight(n)) * inverse * weight(n))
         for g in range(members):
             right_ref[:, pl.ds(g * share, share)] = all_lines[g, 2 * per:2 * per + 1, pl.ds(0, share)]
         arrived(FIRST)
-        cast(0)
-        solve_all(list(range(0, half, LANES)) + [None], 0)
-        schur_ref[pl.ds(0, half), pl.ds(0, half + LANES)] = product(0, 0, half + LANES)
+        solve(0)
+        product(0, half + EXTRA, 0)
         arrived(SECOND)
-        cast(1)
-        solve_all(list(range(half, 2 * half, LANES)), half + LANES)
-        schur_ref[pl.ds(0, half), pl.ds(half + LANES, half)] = product(0, half + LANES, half)
-        schur_ref[pl.ds(half, half), pl.ds(half, half + LANES)] = product(1, half, half + LANES)
+        solve(1)
+        product(half + EXTRA, half, 0)
+        product(half, half + EXTRA, 1)
         arrived(DIAGONAL, LINK)
         for k, other in enumerate(others):
             @pl.when(lax.div(other, members // 2) == lax.div(lead, members // 2))
@@ -381,15 +384,15 @@
     _, times, cells, rows, size = coupling.shape
     share, roots = link.shape[1:]
     per, members, half = times * cells, plan.members, size // 2
-    count, wide = members * per, size + LANES
+    count, wide = members * per, size + EXTRA
     SMEM = pl.BlockSpec(memory_space=pltpu.SMEM)
     lines = -(-(2 * per + 1) // 8) * 8
     shape = lambda *sizes: jax.ShapeDtypeStruct(sizes, F32)
     return pl.pallas_call(
         functools.partial(leaf_kernel, plan, neighbours(plan, times, cells), per),
         out_shape=[
-            shape(size, wide),
-            shape(count, rows, wide),
+            shape(wide, size),
+            shape(wide, count * rows),
             shape(1, size),
             shape(members, share, half),
             shape(members // 2, share, half),
@@ -399,19 +402,18 @@
         out_specs=[VMEM, VMEM, VMEM, ANY, ANY, ANY],
         scratch_shapes=[
             pltpu.VMEM((lines, LANES), F32),
-            pltpu.VMEM((2, per, rows, half), F32),
+            pltpu.VMEM((2, per, half, rows), F32),
             pltpu.VMEM((per, rows, rows), F32),
             pltpu.VMEM((share, half), F32),
             pltpu.VMEM((share, half), F32),
             pltpu.VMEM((share, roots), F32),
             pltpu.VMEM((members, lines, LANES), F32),
-            pltpu.VMEM((2, members, per, rows, half), F32),
+            pltpu.VMEM((2, members, per, half, rows), F32),
             pltpu.VMEM((members, per, rows, rows), F32),
-            pltpu.VMEM((2, count, rows, half + LANES if count <= 8 else LANES), F32),
-            pltpu.VMEM((count, rows, 3 * rows), BF16),
-            pltpu.VMEM((count, rows, 3 * rows), BF16),
-            pltpu.VMEM((count, rows, LANES), F32),
-            pltpu.VMEM((2, count * rows, half), BF16),
+            pltpu.VMEM((2, half + EXTRA, count * rows), F32),
+            pltpu.VMEM((count, 2 * rows, 2 * rows), BF16),
+            pltpu.VMEM((count, 2 * rows, 2 * rows), BF16),
+            pltpu.VMEM((2, half, count * rows), BF16),
             pltpu.SemaphoreType.DMA((7,)),
             pltpu.SemaphoreType.DMA((7, members - 1)),
             pltpu.SemaphoreType.DMA((3,)),
@@ -495,18 +497,7 @@
     )(term)
 
 
-def scatter_kernel(plan, pack_ref, leaf_ref, parent_ref, root_ref, landed, send, receive):
-    times, cells = leaf_ref.shape[1:3]
-    roots, share = root_ref.shape[0], parent_ref.shape[1]
-    base = times * cells * LANES
-
-    def write(line):
-        for k in range(times * cells):
-            t, c = divmod(k, cells)
-            leaf_ref[0, t, c:c + 1, :] = line[:, k * LANES:(k + 1) * LANES]
-        root_ref[...] = line[0, base:base + roots]
-        parent_ref[...] = line[:, base + roots:base + roots + share]
-
+def scatter_kernel(plan, pack_ref, out_ref, landed, send, receive):
     scen, member = plan.here()
     lead = plan.leader(scen)
     barrier = pltpu.get_barrier_semaphore()
@@ -522,7 +513,7 @@
         pl.semaphore_signal(barrier, inc=1, device_id=plan.device(scen, lead), device_id_type=MESH)
         pl.semaphore_wait(barrier, 1)
         remote(0, lead).wait_recv()
-        write(landed[0:1, :])
+        out_ref[...] = landed[...]
 
     @pl.when(member == lead)
     def _():
@@ -535,17 +526,17 @@
         copies = [remote(k, other) for k, other in enumerate(others)]
         for copy in copies:
             copy.start()
-        write(pack_ref[member][0:1, :])
+        out_ref[...] = pack_ref[member]
         for copy in copies:
             copy.wait_send()
 
 
-def scatter(plan, pack, shapes):
+def scatter(plan, pack):
     return pl.pallas_call(
         functools.partial(scatter_kernel, plan),
-        out_shape=[jax.ShapeDtypeStruct(shape, F32) for shape in shapes],
+        out_shape=jax.ShapeDtypeStruct(pack.shape[1:], F32),
         in_specs=[VMEM],
-        out_specs=[VMEM] * 3,
+        out_specs=VMEM,
         scratch_shapes=[
             pltpu.VMEM(pack.shape[1:], F32),
             pltpu.SemaphoreType.DMA((plan.members - 1,)),
@@ -636,7 +627,12 @@
     pack = local_call(
         root_kernel, jax.ShapeDtypeStruct((plan.members, 8, width), F32), 6
     )(root_mat, total, vector, root_rhs[None], solution_p, solved)
-    return scatter(plan, pack, [leaf_rhs.shape, (1, share), (roots,)])
+    shapes = [leaf_rhs.shape, (1, share), (roots,)]
+    return tuple(
+        local_call(finish_kernel, [jax.ShapeDtypeStruct(shape, F32) for shape in shapes], 1)(
+            scatter(plan, pack)
+        )
+    )
 
 
 def solution(mesh):

time: 83.4 us -> 75 us (0.90)
  Pallas kernels: 77 us -> 72.1 us
  local copies, waits for them, and re-layouts: 4.8 us -> 1.3 us
    pallas_call x1 -> x2, Pallas kernels: 30 us -> 25.6 us  [the longest x1 24.3 us: scatter(): pl.pallas_call(functools.partial(scatter_kernel, plan), out_shape=jax.Sha...]
    unnamed x4 -> x1, local copies, waits for them, and re-layouts: 4.8 us -> 1.3 us
where the time goes in v3:
time: 75 us; the launch traced here: 74.7 us
  Pallas kernels  72.1 us (96%)
  local copies, waits for them, and re-layouts  1.3 us (2%)
  between operations  1.3 us (2%)
    pallas_call x1, Pallas kernels, solve_leaves(): pl.pallas_call(functools.partial(leaf_kernel, plan, neighbours(plan, time...  29.1 us
    pallas_call x1, Pallas kernels, scatter(): pl.pallas_call(functools.partial(scatter_kernel, plan), out_shape=jax.Sha...  24.3 us
    pallas_call x1, Pallas kernels, body(): local_call(functools.partial(parent_kernel, plan), [jax.ShapeDtypeStruct(...  8.17 us
    pallas_call x1, Pallas kernels, body(): local_call(root_kernel, jax.ShapeDtypeStruct((plan.members, 8, width), F3...  7.2 us
    pallas_call x1, Pallas kernels, sum_terms(): pl.pallas_call(functools.partial(sum_kernel, plan), out_shape=[jax.ShapeD...  2.04 us

profile of v3, /device:TPU:0, one launch (start us, length us, event | category | flops | bytes accessed | tf_op | source)
XLA Modules:
  0.0 74.7 jit_solution(7163982751242978382)
XLA Ops:
  1.3 1.3 %copy.14.compressor_ref = s32[1,2,1]{2,1,0:T(2,128)} copy(s32[1,2,1]{1,2,0:T(1,128)} %param.14) | data formatting | bytes 16 | tf_op args[3]
  2.6 29.1 %shard_map.130 = (f32[528,512]{1,0:T(8,128)}, f32[528,1024]{1,0:T(8,128)}, f32[1,512]{1,0:T(1,128)}, f32[4,128,256]{2,1,0:T(8,128)}, f32[2,128,256]{2,1,0:T(8,128)}, /*index=5*/f32[4,128,256]{2,1,0:T(8,128)}) custom-call(bf16[1,2,1,128,512]{4,3,2,1,0:T(8,128)(2,1)} %coupling_ref.1, f32[1,2,1,128]{3,2,1,0:T(1,128)} %rhs_ref.1, ...), custom_call_target="tpu_custom_call" | custom-call | tf_op jit(solution)/shard_map/pallas_call | solution.py:391
  31.7 8.2 %shard_map.131 = (f32[512,384]{1,0:T(8,128)}, f32[264,256]{1,0:T(8,128)}) custom-call(f32[528,512]{1,0:T(8,128)} %get-tuple-element.13.schur_ref, f32[512,256]{1,0:T(8,128)} %bitcast.4, f32[256,256]{1,0:T(8,128)} %bitcast.6, f32[1,512]{1,0:T(1,128)} %get-tuple-element.16.right_ref, f32[512,256]{1,0:T(8,128)} %bitcast.5), custom_call_target="tpu_custom_call" | custom-call | tf_op jit(solution)/shard_map/pallas_call | solution.py:609
  39.9 2.0 %shard_map.132 = (f32[256,256]{1,0:T(8,128)}, f32[8,256]{1,0:T(8,128)}) custom-call(f32[264,256]{1,0:T(8,128)} %get-tuple-element.18.term_ref), custom_call_target="tpu_custom_call" | custom-call | tf_op jit(solution)/shard_map/pallas_call | solution.py:484
  41.9 7.2 %shard_map.133.pack_ref = f32[4,8,640]{2,1,0:T(8,128)} custom-call(f32[256,256]{1,0:T(8,128)} %matrix_ref.1, f32[256,256]{1,0:T(8,128)} %get-tuple-element.19.term_ref, f32[8,256]{1,0:T(8,128)} %get-tuple-element.20.vector_ref, f32[1,256]{1,0:T(1,128)} %bitcast.7, f32[512,384]{1,0:T(8,128)} %get-tuple-element.21.solution_ref, ...), custom_call_target="tpu_custom_call" | custom-call | tf_op jit(solution)/shard_map/pallas_call | solution.py:627
  49.1 24.3 %shard_map.134.line_ref = f32[8,640]{1,0:T(8,128)} custom-call(f32[4,8,640]{2,1,0:T(8,128)} %shard_map.133.pack_ref), custom_call_target="tpu_custom_call" | custom-call | tf_op jit(solution)/shard_map/pallas_call | solution.py:535
  73.4 1.3 %shard_map.135 = (f32[1,2,1,128]{3,2,1,0:T(1,128)}, f32[1,128]{1,0:T(1,128)}, f32[256]{0:T(256)}) custom-call(f32[8,640]{1,0:T(8,128)} %shard_map.134.line_ref), custom_call_target="tpu_custom_call" | custom-call | tf_op jit(solution)/shard_map/pallas_call | solution.py:632

commit v4 on v3

--- a/solution.py
+++ b/solution.py
@@ -67,7 +67,8 @@
         return x + both[:size], both[size:]
 
     def correct(_, x):
-        return x + near_dot(x, identity - full_dot(matrix, x))
+        left = identity - full_dot(matrix, x)
+        return x + fast_dot(x.astype(BF16), left.astype(BF16))
 
     if steps is not None:
         x, _ = lax.fori_loop(0, steps, lambda _, state: grow(*state), (start, residual))
@@ -91,8 +92,10 @@
     return steps
 
 
-def parent_kernel(plan, schur_ref, diagonal_ref, beside_ref, right_ref, link_ref, solution_ref, term_ref):
-    half = diagonal_ref.shape[1]
+def parent_kernel(plan, schur_ref, corner_ref, diagonal_ref, beside_ref, right_ref, link_ref,
+                  solution_ref, term_ref):
+    part = diagonal_ref.shape[1]
+    half = 2 * part
     size = 2 * half
     roots = link_ref.shape[1]
     scen, _ = plan.here()
@@ -105,21 +108,38 @@
     behind = pl.ds(half + EXTRA, half)
     sides = jnp.concatenate([link_ref[...], right], axis=1)
     beside = beside_ref[...]
-    h11 = diagonal_ref[a, :] + schur_ref[a, a]
+
+    def diagonal(start):
+        upper = jnp.concatenate(
+            [corner_ref[pl.ds(start, part), :], diagonal_ref[pl.ds(start, part), :]], axis=1
+        )
+        lower = jnp.concatenate(
+            [upper[:, part:].T, diagonal_ref[pl.ds(start + part, part), :]], axis=1
+        )
+        return jnp.concatenate([upper, lower], axis=0)
+
+    h11 = diagonal(0) + schur_ref[a, a]
     h21 = jnp.where(near == 0, beside.T, beside) + schur_ref[behind, a]
-    h22 = diagonal_ref[b, :] + schur_ref[behind, b]
+    h22 = diagonal(half) + schur_ref[behind, b]
     x11 = spd_inverse(h11)
     across = full_dot(x11, h21, NT)
-    ahead = full_dot(x11, sides[:half])
+    ahead = near_dot(x11, sides[:half])
     x22 = spd_inverse(h22 - full_dot(h21, across))
-    lower = near_dot(x22, sides[half:] - full_dot(h21, ahead))
+    lower = near_dot(x22, sides[half:] - near_dot(h21, ahead))
     upper = ahead - near_dot(across, lower)
     solution_ref[a, :] = upper
     solution_ref[b, :] = lower
     term_ref[...] = near_dot(solution_ref[...], link_ref[...], TN)[:roots + 8]
 
 
-def root_kernel(matrix_ref, term_ref, vector_ref, right_ref, solution_ref, solved_ref, pack_ref):
+def root_kernel(matrix_ref, term_ref, vector_ref, right_ref, solution_any, solved_any, pack_ref,
+                solution_ref, solved_ref, local):
+    loads = [
+        pltpu.make_async_copy(solution_any, solution_ref, local.at[0]),
+        pltpu.make_async_copy(solved_any, solved_ref, local.at[1]),
+    ]
+    for load in loads:
+        load.start()
     roots = matrix_ref.shape[0]
     size = solution_ref.shape[0]
     groups = pack_ref.shape[0]
@@ -128,6 +148,8 @@
     share = size // groups
     inverse = spd_inverse(matrix_ref[...] + term_ref[...])
     root = full_dot(right_ref[...] - vector_ref[...], inverse)
+    for load in loads:
+        load.wait()
     lane = lax.broadcasted_iota(jnp.int32, (8, LANES), 1)
     unit = jnp.where(lane == 0, 1.0, 0.0).astype(F32)
     parent = full_dot(jnp.concatenate([root, unit], axis=1), solution_ref[...], NT)
@@ -174,12 +196,14 @@
 
 def leaf_kernel(plan, beside, per, coupling_ref, rhs_ref, conductance_ref, compressor_ref, blocks_ref,
                 parent_of_ref, parent_mat_ref, parent_rhs_ref, link_ref,
-                schur_ref, solved_ref, right_ref, all_diagonal, all_beside, all_link,
-                own_lines, own_half, own_inverse, own_diagonal, own_beside, own_link,
+                schur_ref, solved_ref, right_ref, all_corner, all_diagonal, all_beside, all_link,
+                own_lines, own_half, own_inverse, own_corner, own_diagonal, own_beside, own_link,
+                mats, links, own_diag, all_diag,
                 all_lines, all_half, all_inverse,
                 field, plain, scaled, bits, send, receive, local):
     count = len(beside)
     members = plan.members
+    packed = per % 2 == 0
     times, cells = coupling_ref.shape[1:3]
     half = coupling_ref.shape[-1] // 2
     share = parent_rhs_ref.shape[1]
@@ -189,7 +213,15 @@
     close = lax.div(member, members // 2) == lax.div(lead, members // 2)
     place = lax.rem(member, members // 2)
     barrier = pltpu.get_barrier_semaphore()
-    LINES, FIRST, INVERSE, SECOND, DIAGONAL, LINK, BESIDE = range(7)
+    LINES, FIRST, INVERSE, SECOND, DIAGONAL, LINK, BESIDE, CORNER, DIAG = range(9)
+    part = half // 2
+    cornered = place * share < part
+    loads = [
+        pltpu.make_async_copy(parent_mat_ref, mats, local.at[4]),
+        pltpu.make_async_copy(link_ref, links, local.at[5]),
+    ]
+    for load in loads:
+        load.start()
 
     def remote(kind, at, slot):
         source, target = {
@@ -198,6 +230,8 @@
             INVERSE: (own_inverse, all_inverse.at[at]),
             SECOND: (own_half.at[1], all_half.at[1, at]),
             DIAGONAL: (own_diagonal, all_diagonal.at[at]),
+            CORNER: (own_corner, all_corner.at[at]),
+            DIAG: (own_diag, all_diag.at[at]),
             LINK: (own_link, all_link.at[at]),
             BESIDE: (own_beside, all_beside.at[lax.rem(at, members // 2)]),
         }[kind]
@@ -222,6 +256,7 @@
 
     label = parent_of_ref[0]
     own_lines[...] = jnp.zeros_like(own_lines)
+    own_diag[...] = jnp.zeros_like(own_diag)
     for k in range(per):
         t, c = divmod(k, cells)
         own_lines[k:k + 1, :] = rhs_ref[0, t, c:c + 1, :]
@@ -247,22 +282,39 @@
             [jnp.concatenate([first, zero], axis=1), jnp.concatenate([zero, second], axis=1)], axis=0
         )
         found = spd_inverse(pair, steps_for(8.0 * rows))
-        own_inverse[i] = found[:rows, :rows]
-        own_inverse[j] = found[rows:, rows:]
-    strip = parent_mat_ref[label]
+        if packed:
+            row = lax.broadcasted_iota(jnp.int32, (rows, rows), 0)
+            column = lax.broadcasted_iota(jnp.int32, (rows, rows), 1)
+            own_inverse[i // 2] = jnp.where(row <= column, found[:rows, :rows], found[rows:, rows:])
+            kept = jnp.where(row == column, found[rows:, rows:], 0.0)
+            own_diag[i // 2:i // 2 + 1, :] = jnp.sum(kept, axis=0, keepdims=True)
+        else:
+            own_inverse[i] = found[:rows, :rows]
+            own_inverse[j] = found[rows:, rows:]
+    for load in loads:
+        load.wait()
+    strip = mats[label]
     lower = lax.div(member, members // 2) == 0
-    own_diagonal[...] = jnp.where(lower, strip[:, :half], strip[:, half:])
+    square = jnp.where(lower, strip[:, :half], strip[:, half:])
+    own_corner[...] = square[:, :part]
+    own_diagonal[...] = square[:, part:]
     own_beside[...] = jnp.where(lower, strip[:, half:], strip[:, :half])
-    own_link[...] = link_ref[label]
+    own_link[...] = links[label]
 
     @pl.when(jnp.logical_not(leads))
     def _():
         remote(INVERSE, member, slot).start()
+        remote(DIAG, member, slot).start()
         remote(SECOND, member, slot).start()
-        for kind in (LINES, FIRST, INVERSE, SECOND):
+        for kind in (LINES, FIRST, INVERSE, DIAG, SECOND):
             remote(kind, member, slot).wait_send()
         remote(DIAGONAL, member, slot).start()
         remote(LINK, member, slot).start()
+
+        @pl.when(cornered)
+        def _():
+            remote(CORNER, member, slot).start()
+            remote(CORNER, member, slot).wait_send()
 
         @pl.when(close)
         def _():
@@ -276,6 +328,18 @@
         for kind in kinds:
             for k, other in enumerate(others):
                 remote(kind, other, k).wait_recv()
+
+    def unpacked(g, k):
+        if not packed:
+            return all_inverse[g, k]
+        both = all_inverse[g, k // 2]
+        other = both.T
+        row = lax.broadcasted_iota(jnp.int32, both.shape, 0)
+        column = lax.broadcasted_iota(jnp.int32, both.shape, 1)
+        if k % 2 == 0:
+            return jnp.where(row <= column, both, other)
+        middle = jnp.broadcast_to(all_diag[g, k // 2:k // 2 + 1, :], both.shape)
+        return jnp.where(row > column, both, jnp.where(row < column, other, middle))
 
     def tile(matrix):
         top, low = halves(matrix)
@@ -347,18 +411,20 @@
             pltpu.make_async_copy(own_diagonal, all_diagonal.at[member], local.at[0]),
             pltpu.make_async_copy(own_link, all_link.at[member], local.at[1]),
             pltpu.make_async_copy(own_beside, all_beside.at[place], local.at[2]),
+            pltpu.make_async_copy(own_corner, all_corner.at[member], local.at[3]),
         ]
         for copy in own:
             copy.start()
         all_lines[member] = own_lines[...]
         all_inverse[member] = own_inverse[...]
+        all_diag[member] = own_diag[...]
         for j in range(2):
             all_half[j, member] = own_half[j]
         pl.semaphore_wait(barrier, members - 1)
-        arrived(LINES, INVERSE)
+        arrived(LINES, INVERSE, DIAG)
         for n in range(count):
             g, k = divmod(n, per)
-            inverse = all_inverse[g, k]
+            inverse = unpacked(g, k)
             plain[n] = tile(inverse)
             scaled[n] = tile(as_columns(weight(n)) * inverse * weight(n))
         for g in range(members):
@@ -375,6 +441,11 @@
             @pl.when(lax.div(other, members // 2) == lax.div(lead, members // 2))
             def _():
                 remote(BESIDE, other, k).wait_recv()
+
+            @pl.when(lax.rem(other, members // 2) * share < part)
+            def _():
+                remote(CORNER, other, k).wait_recv()
+
         for copy in own:
             copy.wait()
 
@@ -387,6 +458,7 @@
     count, wide = members * per, size + EXTRA
     SMEM = pl.BlockSpec(memory_space=pltpu.SMEM)
     lines = -(-(2 * per + 1) // 8) * 8
+    blocks_sent = per if per % 2 else per // 2
     shape = lambda *sizes: jax.ShapeDtypeStruct(sizes, F32)
     return pl.pallas_call(
         functools.partial(leaf_kernel, plan, neighbours(plan, times, cells), per),
@@ -394,29 +466,35 @@
             shape(wide, size),
             shape(wide, count * rows),
             shape(1, size),
-            shape(members, share, half),
+            shape(members, share, half // 2),
+            shape(members, share, half // 2),
             shape(members // 2, share, half),
             shape(members, share, roots),
         ],
-        in_specs=[VMEM, VMEM, VMEM, SMEM, VMEM, SMEM, VMEM, VMEM, VMEM],
-        out_specs=[VMEM, VMEM, VMEM, ANY, ANY, ANY],
+        in_specs=[VMEM, VMEM, VMEM, SMEM, VMEM, SMEM, ANY, VMEM, ANY],
+        out_specs=[VMEM, VMEM, VMEM, ANY, ANY, ANY, ANY],
         scratch_shapes=[
             pltpu.VMEM((lines, LANES), F32),
             pltpu.VMEM((2, per, half, rows), F32),
-            pltpu.VMEM((per, rows, rows), F32),
-            pltpu.VMEM((share, half), F32),
+            pltpu.VMEM((blocks_sent, rows, rows), F32),
+            pltpu.VMEM((share, half // 2), F32),
+            pltpu.VMEM((share, half // 2), F32),
             pltpu.VMEM((share, half), F32),
             pltpu.VMEM((share, roots), F32),
+            pltpu.VMEM(parent_mat.shape, F32),
+            pltpu.VMEM(link.shape, F32),
+            pltpu.VMEM((8 * -(-per // 16), LANES), F32),
+            pltpu.VMEM((members, 8 * -(-per // 16), LANES), F32),
             pltpu.VMEM((members, lines, LANES), F32),
             pltpu.VMEM((2, members, per, half, rows), F32),
-            pltpu.VMEM((members, per, rows, rows), F32),
+            pltpu.VMEM((members, blocks_sent, rows, rows), F32),
             pltpu.VMEM((2, half + EXTRA, count * rows), F32),
             pltpu.VMEM((count, 2 * rows, 2 * rows), BF16),
             pltpu.VMEM((count, 2 * rows, 2 * rows), BF16),
             pltpu.VMEM((2, half, count * rows), BF16),
-            pltpu.SemaphoreType.DMA((7,)),
-            pltpu.SemaphoreType.DMA((7, members - 1)),
-            pltpu.SemaphoreType.DMA((3,)),
+            pltpu.SemaphoreType.DMA((9,)),
+            pltpu.SemaphoreType.DMA((9, members - 1)),
+            pltpu.SemaphoreType.DMA((6,)),
         ],
         compiler_params=pltpu.CompilerParams(
             collective_id=0, has_side_effects=True, vmem_limit_bytes=LIMIT
@@ -546,12 +624,12 @@
     )(pack)
 
 
-def local_call(kernel, out_shape, count, scratch=()):
+def local_call(kernel, out_shape, count, scratch=(), outside=0):
     many = isinstance(out_shape, list)
     return pl.pallas_call(
         kernel,
         out_shape=out_shape,
-        in_specs=[VMEM] * count,
+        in_specs=[VMEM] * (count - outside) + [ANY] * outside,
         out_specs=[VMEM] * len(out_shape) if many else VMEM,
         scratch_shapes=list(scratch),
         compiler_params=pltpu.CompilerParams(vmem_limit_bytes=LIMIT),
@@ -600,7 +678,7 @@
     per = times * cells
     roots = root_rhs.shape[0]
     share = parent_rhs.shape[1]
-    schur, solved, right, diagonal, beside, all_link = solve_leaves(
+    schur, solved, right, corner, diagonal, beside, all_link = solve_leaves(
         plan,
         [coupling, leaf_rhs, conductance, compressor, blocks, parent_of, parent_mat, parent_rhs, link],
     )
@@ -612,10 +690,11 @@
             jax.ShapeDtypeStruct((size, roots + LANES), F32),
             jax.ShapeDtypeStruct((roots + 8, roots), F32),
         ],
-        5,
+        6,
     )(
         schur,
-        diagonal.reshape(size, size // 2),
+        corner.reshape(size, size // 4),
+        diagonal.reshape(size, size // 4),
         beside.reshape(size // 2, size // 2),
         right,
         all_link.reshape(size, roots),
@@ -625,7 +704,15 @@
     total, vector = sum_terms(plan, term)
     width = per * rows + roots + -(-share // LANES) * LANES
     pack = local_call(
-        root_kernel, jax.ShapeDtypeStruct((plan.members, 8, width), F32), 6
+        root_kernel,
+        jax.ShapeDtypeStruct((plan.members, 8, width), F32),
+        6,
+        [
+            pltpu.VMEM(solution_p.shape, F32),
+            pltpu.VMEM(solved.shape, F32),
+            pltpu.SemaphoreType.DMA((2,)),
+        ],
+        2,
     )(root_mat, total, vector, root_rhs[None], solution_p, solved)
     shapes = [leaf_rhs.shape, (1, share), (roots,)]
     return tuple(

time: 75 us -> 71 us (0.947)
  Pallas kernels: 72.1 us -> 68.1 us
    pallas_call x1, Pallas kernels: 29.1 us -> 26.5 us  [solve_leaves(): pl.pallas_call(functools.partial(leaf_kernel, plan, neighbours(plan, time...]
    pallas_call x1, Pallas kernels: 7.2 us -> 6.07 us  [body(): local_call(root_kernel, jax.ShapeDtypeStruct((plan.members, 8, width), F3...]
where the time goes in v4:
time: 71 us; the launch traced here: 70.7 us
  Pallas kernels  68.1 us (96%)
  between operations  1.31 us (2%)
  local copies, waits for them, and re-layouts  1.3 us (2%)
    pallas_call x1, Pallas kernels, solve_leaves(): pl.pallas_call(functools.partial(leaf_kernel, plan, neighbours(plan, time...  26.5 us
    pallas_call x1, Pallas kernels, scatter(): pl.pallas_call(functools.partial(scatter_kernel, plan), out_shape=jax.Sha...  24.8 us
    pallas_call x1, Pallas kernels, body(): local_call(functools.partial(parent_kernel, plan), [jax.ShapeDtypeStruct(...  7.44 us
    pallas_call x1, Pallas kernels, body(): local_call(root_kernel, jax.ShapeDtypeStruct((plan.members, 8, width), F3...  6.07 us
    pallas_call x1, Pallas kernels, sum_terms(): pl.pallas_call(functools.partial(sum_kernel, plan), out_shape=[jax.ShapeD...  2.04 us

profile of v4, /device:TPU:0, one launch (start us, length us, event | category | flops | bytes accessed | tf_op | source)
XLA Modules:
  0.0 70.7 jit_solution(3256836337109649813)
XLA Ops:
  1.3 1.3 %copy.14.compressor_ref = s32[1,2,1]{2,1,0:T(2,128)} copy(s32[1,2,1]{1,2,0:T(1,128)} %param.14) | data formatting | bytes 16 | tf_op args[3]
  2.6 26.5 %shard_map.130 = (f32[528,512]{1,0:T(8,128)}, f32[528,1024]{1,0:T(8,128)}, f32[1,512]{1,0:T(1,128)}, f32[4,128,128]{2,1,0:T(8,128)}, f32[4,128,128]{2,1,0:T(8,12...) custom-call(bf16[1,2,1,128,512]{4,3,2,1,0:T(8,128)(2,1)} %coupling_ref.1, f32[1,2,1,128]{3,2,1,0:T(1,128)} %rhs_ref.1, ...), custom_call_target="tpu_custom_call" | custom-call | tf_op jit(solution)/shard_map/pallas_call | solution.py:463
  29.1 7.4 %shard_map.131 = (f32[512,384]{1,0:T(8,128)}, f32[264,256]{1,0:T(8,128)}) custom-call(f32[528,512]{1,0:T(8,128)} %get-tuple-element.14.schur_ref, f32[512,128]{1,0:T(8,128)} %bitcast.6, f32[512,128]{1,0:T(8,128)} %bitcast.7, f32[256,256]{1,0:T(8,128)} %bitcast.8, f32[1,512]{1,0:T(1,128)} %get-tuple-element.18.right_ref, f32[512,256]{1,0:T(8,128)} %bitcast.5), custom_call_target="tpu_custom_call" | custom-call | tf_op jit(solution)/shard_map/pallas_call | solution.py:687
  36.5 2.0 %shard_map.132 = (f32[256,256]{1,0:T(8,128)}, f32[8,256]{1,0:T(8,128)}) custom-call(f32[264,256]{1,0:T(8,128)} %get-tuple-element.20.term_ref), custom_call_target="tpu_custom_call" | custom-call | tf_op jit(solution)/shard_map/pallas_call | solution.py:562
  38.6 6.1 %shard_map.133.pack_ref = f32[4,8,640]{2,1,0:T(8,128)} custom-call(f32[256,256]{1,0:T(8,128)} %matrix_ref.1, f32[256,256]{1,0:T(8,128)} %get-tuple-element.21.term_ref, f32[8,256]{1,0:T(8,128)} %get-tuple-element.22.vector_ref, f32[1,256]{1,0:T(1,128)} %bitcast.9, f32[512,384]{1,0:T(8,128)} %get-tuple-element.23.solution_any, ...), custom_call_target="tpu_custom_call" | custom-call | tf_op jit(solution)/shard_map/pallas_call | solution.py:706
  44.6 24.8 %shard_map.134.line_ref = f32[8,640]{1,0:T(8,128)} custom-call(f32[4,8,640]{2,1,0:T(8,128)} %shard_map.133.pack_ref), custom_call_target="tpu_custom_call" | custom-call | tf_op jit(solution)/shard_map/pallas_call | solution.py:613
  69.4 1.3 %shard_map.135 = (f32[1,2,1,128]{3,2,1,0:T(1,128)}, f32[1,128]{1,0:T(1,128)}, f32[256]{0:T(256)}) custom-call(f32[8,640]{1,0:T(8,128)} %shard_map.134.line_ref), custom_call_target="tpu_custom_call" | custom-call | tf_op jit(solution)/shard_map/pallas_call | solution.py:719

commit v5 on v4

--- a/solution.py
+++ b/solution.py
@@ -16,7 +16,7 @@
 MESH = pl.DeviceIdType.MESH
 VMEM = pl.BlockSpec(memory_space=pltpu.VMEM)
 ANY = pl.BlockSpec(memory_space=pl.ANY)
-LIMIT = 56 * 1024 * 1024
+MIB = 1024 * 1024
 SETTLED = 3e-4
 EXTRA = 16
 NN = ((1,), (0,))
@@ -497,7 +497,9 @@
             pltpu.SemaphoreType.DMA((6,)),
         ],
         compiler_params=pltpu.CompilerParams(
-            collective_id=0, has_side_effects=True, vmem_limit_bytes=LIMIT
+            collective_id=0,
+            has_side_effects=True,
+            vmem_limit_bytes=(28 if count <= 8 else 56) * MIB,
         ),
     )(*arrays)
 
@@ -624,7 +626,7 @@
     )(pack)
 
 
-def local_call(kernel, out_shape, count, scratch=(), outside=0):
+def local_call(kernel, out_shape, count, scratch=(), outside=0, limit=24 * MIB):
     many = isinstance(out_shape, list)
     return pl.pallas_call(
         kernel,
@@ -632,7 +634,7 @@
         in_specs=[VMEM] * (count - outside) + [ANY] * outside,
         out_specs=[VMEM] * len(out_shape) if many else VMEM,
         scratch_shapes=list(scratch),
-        compiler_params=pltpu.CompilerParams(vmem_limit_bytes=LIMIT),
+        compiler_params=pltpu.CompilerParams(vmem_limit_bytes=limit),
     )
 
 
@@ -713,6 +715,7 @@
             pltpu.SemaphoreType.DMA((2,)),
         ],
         2,
+        (16 if plan.members <= 4 else 32) * MIB,
     )(root_mat, total, vector, root_rhs[None], solution_p, solved)
     shapes = [leaf_rhs.shape, (1, share), (roots,)]
     return tuple(

time: 71 us -> 74.4 us (1.048)
  local copies, waits for them, and re-layouts: 1.3 us -> 11.1 us
  Pallas kernels: 68.1 us -> 61.3 us
    unnamed x1 -> x29, local copies, waits for them, and re-layouts: 1.3 us -> 11.1 us
    pallas_call x1, Pallas kernels: 7.44 us -> 5.08 us  [body(): local_call(functools.partial(parent_kernel, plan), [jax.ShapeDtypeStruct(...]
    pallas_call x1, Pallas kernels: 26.5 us -> 24.5 us  [solve_leaves(): pl.pallas_call(functools.partial(leaf_kernel, plan, neighbours(plan, time...]
    pallas_call x1, Pallas kernels: 6.07 us -> 4.69 us  [body(): local_call(root_kernel, jax.ShapeDtypeStruct((plan.members, 8, width), F3...]
where the time goes in v5:
time: 74.4 us; the launch traced here: 73.9 us
  Pallas kernels  61.3 us (82%)
  local copies, waits for them, and re-layouts  11.1 us (15%)
  between operations  1.39 us (2%)
    pallas_call x1, Pallas kernels, solve_leaves(): pl.pallas_call(functools.partial(leaf_kernel, plan, neighbours(plan, time...  24.5 us
    pallas_call x1, Pallas kernels, scatter(): pl.pallas_call(functools.partial(scatter_kernel, plan), out_shape=jax.Sha...  24.4 us
    unnamed x29, local copies, waits for them, and re-layouts  11.1 us
    pallas_call x1, Pallas kernels, body(): local_call(functools.partial(parent_kernel, plan), [jax.ShapeDtypeStruct(...  5.08 us
    pallas_call x1, Pallas kernels, body(): local_call(root_kernel, jax.ShapeDtypeStruct((plan.members, 8, width), F3...  4.69 us
    pallas_call x1, Pallas kernels, sum_terms(): pl.pallas_call(functools.partial(sum_kernel, plan), out_shape=[jax.ShapeD...  2.05 us

profile of v5, /device:TPU:0, one launch (start us, length us, event | category | flops | bytes accessed | tf_op | source)
XLA Modules:
  0.0 73.9 jit_solution(8381902630812513256)
XLA Ops:
  1.3 0.7 %copy.14.compressor_ref = s32[1,2,1]{2,1,0:T(2,128)S(1)} copy(s32[1,2,1]{1,2,0:T(1,128)} %param.14) | data formatting | bytes 16 | tf_op args[3]
  2.0 1.6 %copy-done = f32[8,128,512]{2,1,0:T(8,128)S(1)} copy-done((f32[8,128,512]{2,1,0:T(8,128)S(1)}, f32[8,128,512]{2,1,0:T(8,128)}, u32[]{:S(2)}) %copy-start) | copy-done | bytes 2097176
  3.6 1.2 %copy-done.1 = f32[8,128,256]{2,1,0:T(8,128)S(1)} copy-done((f32[8,128,256]{2,1,0:T(8,128)S(1)}, f32[8,128,256]{2,1,0:T(8,128)}, u32[]{:S(2)}) %copy-start.1) | copy-done | bytes 1048600
  4.8 0.9 %copy-done.4 = bf16[1,2,1,128,512]{4,3,2,1,0:T(8,128)(2,1)S(1)} copy-done((bf16[1,2,1,128,512]{4,3,2,1,0:T(8,128)(2,1)S(1)}, bf16[1,2,1,128,512]{4,3,2,1,0:T(8,128)(2,1)}, u32[]{:S(2)}) %copy-start.4) | copy-done | bytes 262168
  5.8 0.9 %copy-done.7 = f32[1,2,1,128,128]{4,3,2,1,0:T(8,128)S(1)} copy-done((f32[1,2,1,128,128]{4,3,2,1,0:T(8,128)S(1)}, f32[1,2,1,128,128]{4,3,2,1,0:T(8,128)}, u32[]{:S(2)}) %copy-start.7) | copy-done | bytes 131096
  6.7 0.7 copy-done.10
  7.4 0.7 copy-done.11
  8.1 0.7 copy-done.12
  8.7 24.5 %shard_map.130 = (f32[528,512]{1,0:T(8,128)S(1)}, f32[528,1024]{1,0:T(8,128)S(1)}, f32[1,512]{1,0:T(1,128)S(1)}, f32[4,128,128]{2,1,0:T(8,128)S(1)}, f32[4,128,1...) custom-call(bf16[1,2,1,128,512]{4,3,2,1,0:T(8,128)(2,1)S(1)} %copy-done.4, ...), custom_call_target="tpu_custom_call" | custom-call | tf_op jit(solution)/shard_map/pallas_call | solution.py:463
  33.3 0.0 copy-start.5
  33.3 0.0 copy-start.13
  33.3 5.1 %shard_map.131 = (f32[512,384]{1,0:T(8,128)S(1)}, f32[264,256]{1,0:T(8,128)S(1)}) custom-call(f32[528,512]{1,0:T(8,128)S(1)} %get-tuple-element.14.schur_ref, f32[512,128]{1,0:T(8,128)S(1)} %bitcast.6, f32[512,128]{1,0:T(8,128)S(1)} %bitcast.7, f32[256,256]{1,0:T(8,128)S(1)} %bitcast.8, f32[1,512]{1,0:T(1,128)S(1)} %get-tuple-element.18.right_ref, ...), custom_call_target="tpu_custom_call" | custom-call | tf_op jit(solution)/shard_map/pallas_call | solution.py:689
  38.4 0.0 copy-start.3
  38.4 0.7 copy-done.3
  39.1 2.1 %shard_map.132 = (f32[256,256]{1,0:T(8,128)}, f32[8,256]{1,0:T(8,128)}) custom-call(f32[264,256]{1,0:T(8,128)} %copy-done.3), custom_call_target="tpu_custom_call" | custom-call | tf_op jit(solution)/shard_map/pallas_call | solution.py:564
  41.1 0.0 copy-done.5
  41.1 0.0 copy-done.13
  41.2 0.9 %copy-done.6 = f32[256,256]{1,0:T(8,128)S(1)} copy-done((f32[256,256]{1,0:T(8,128)S(1)}, f32[256,256]{1,0:T(8,128)}, u32[]{:S(2)}) %copy-start.6) | copy-done | bytes 262168
  42.1 0.7 copy-done.9
  42.8 4.7 %shard_map.133.pack_ref = f32[4,8,640]{2,1,0:T(8,128)S(1)} custom-call(f32[256,256]{1,0:T(8,128)S(1)} %copy-done.5, f32[256,256]{1,0:T(8,128)S(1)} %copy-done.6, f32[8,256]{1,0:T(8,128)S(1)} %copy-done.9, f32[1,256]{1,0:T(1,128)S(1)} %bitcast.9, f32[512,384]{1,0:T(8,128)S(1)} %get-tuple-element.23.solution_any, f32[528,1024]{1,0:T(8,128)S(1)} %get-tuple-element.24.solved_any), custom_call_target="tpu_custom_call" | custom-call | tf_op jit(solution)/shard_map/pallas_call | solution.py:708
  47.5 0.6 copy-done.2
  48.1 24.4 %shard_map.134.line_ref = f32[8,640]{1,0:T(8,128)} custom-call(f32[4,8,640]{2,1,0:T(8,128)} %copy-done.2), custom_call_target="tpu_custom_call" | custom-call | tf_op jit(solution)/shard_map/pallas_call | solution.py:615
  72.6 0.7 copy-done.8
  73.3 0.6 shard_map.135
  (11 shorter events, 0.0 us)
Async XLA Ops:
  2.0 1.6 %copy-start = (f32[8,128,512]{2,1,0:T(8,128)S(1)}, f32[8,128,512]{2,1,0:T(8,128)}, u32[]{:S(2)}) copy-start(f32[8,128,512]{2,1,0:T(8,128)} %parent_mat_ref.1) | copy-start | bytes 6291460
  3.6 1.2 %copy-start.1 = (f32[8,128,256]{2,1,0:T(8,128)S(1)}, f32[8,128,256]{2,1,0:T(8,128)}, u32[]{:S(2)}) copy-start(f32[8,128,256]{2,1,0:T(8,128)} %link_ref.1) | copy-start | bytes 3145732
  4.8 0.9 %copy-start.4 = (bf16[1,2,1,128,512]{4,3,2,1,0:T(8,128)(2,1)S(1)}, bf16[1,2,1,128,512]{4,3,2,1,0:T(8,128)(2,1)}, u32[]{:S(2)}) copy-start(bf16[1,2,1,128,512]{4,3,2,1,0:T(8,128)(2,1)} %coupling_ref.1) | copy-start | bytes 786436
  5.8 0.9 %copy-start.7 = (f32[1,2,1,128,128]{4,3,2,1,0:T(8,128)S(1)}, f32[1,2,1,128,128]{4,3,2,1,0:T(8,128)}, u32[]{:S(2)}) copy-start(f32[1,2,1,128,128]{4,3,2,1,0:T(8,128)} %blocks_ref.1) | copy-start | bytes 393220
  6.7 0.7 copy-start.10
  7.4 0.7 copy-start.11
  8.1 0.7 copy-start.12
  33.3 7.9 %copy-start.5 = (f32[256,256]{1,0:T(8,128)S(1)}, f32[256,256]{1,0:T(8,128)}, u32[]{:S(2)}) copy-start(f32[256,256]{1,0:T(8,128)} %matrix_ref.1) | copy-start | bytes 786436
  33.3 7.9 %copy-start.13 = (f32[256]{0:T(256)S(1)}, f32[256]{0:T(256)}, u32[]{:S(2)}) copy-start(f32[256]{0:T(256)} %param.21) | copy-start | bytes 3076
  38.4 0.7 copy-start.3
  41.2 1.0 %copy-start.6 = (f32[256,256]{1,0:T(8,128)S(1)}, f32[256,256]{1,0:T(8,128)}, u32[]{:S(2)}) copy-start(f32[256,256]{1,0:T(8,128)} %get-tuple-element.21.term_ref) | copy-start | bytes 786436
  42.1 0.7 copy-start.9
  47.5 0.6 copy-start.2
  72.6 0.7 copy-start.8
